TPU v7x, 32 devices: a whole 2x2x4 slice. The times are simulated.
32 devices in a mesh: seq: 8 (over z, y), head: 4 (over x, core).
Axes of the slice: x: 2, y: 2, z: 4, core: 2. Of those that a mesh axis runs over, the one named last changes fastest.
Arguments:
- queries: bfloat16 [8192, 2048], P('seq', 'head'), may hold values from -11 to 11
- keys_values: bfloat16 [8192, 2, 2048], P('seq', None, 'head'), may hold values from -6 to 6
- rand_blocks: int32 [128, 2], P('seq'), may hold values from 0 to 127, as said below
- w_out: bfloat16 [2048, 4096], P('head'), may hold values from -1 to 1
Outputs:
- mixed: bfloat16 [8192, 4096], P(('seq', 'head'))
Inputs may be any that keep to these rules, and one draw needn't show every extreme that they name: `rand_blocks`: of the 32 entries in the rows of one index of seq, at most 4 name blocks o * 16 to o * 16 + 15 of any one index o; in every draw the blocks of some index o are named exactly 4 times from the rows of every index.
All inputs are finite; a program needn't handle non-finite values.
Results may differ from a plain program's by a relative error of at most 0.013.
Values may be sent and summed in bfloat16 or wider, within the bound.
A program may use at most 128 MiB of HBM per device.

v0:
```python
from functools import reduce

import jax
import jax.numpy as jnp
from jax import lax
from jax.sharding import PartitionSpec as P

HEAD_DIM = 128
BLOCK = 64


def with_halo(cells, sides, width):
    for axis, dim in sides:
        count = lax.axis_size(axis)
        ends = count - 1
        head = lax.slice_in_dim(cells, 0, width, axis=dim)
        tail = lax.slice_in_dim(cells, cells.shape[dim] - width, cells.shape[dim], axis=dim)
        cells = jnp.concatenate(
            [
                lax.ppermute(tail, axis, [(i, (i + 1) % count) for i in range(ends)]),
                cells,
                lax.ppermute(head, axis, [((i + 1) % count, i) for i in range(ends)]),
            ],
            axis=dim,
        )
    return cells


def spread(array, axis, root):
    mine = lax.axis_index(axis) == root
    return lax.psum(jnp.where(mine, array, jnp.zeros_like(array)), axis)


def fetch_random(keys_values, rand_blocks, blocks_dev, seq_count):
    entries = rand_blocks.shape[0] * rand_blocks.shape[1]
    feat_dev = keys_values.shape[2]
    slots = max(1, entries // seq_count)
    flat = rand_blocks.reshape(entries)
    owner = flat // blocks_dev
    offset = flat % blocks_dev
    earlier = jnp.arange(entries)[:, None] > jnp.arange(entries)[None, :]
    rank = jnp.sum((owner[:, None] == owner[None, :]) & earlier, axis=1)
    slot = owner * slots + rank
    placed = slot[:, None] == jnp.arange(seq_count * slots)[None, :]
    outgoing = jnp.sum(jnp.where(placed, offset[:, None], 0), axis=0)
    wanted = lax.all_to_all(
        outgoing.reshape(seq_count, slots), "seq", split_axis=0, concat_axis=0, tiled=True
    )
    local_blocks = keys_values.reshape(blocks_dev, BLOCK, 2, feat_dev)
    answers = local_blocks[wanted]
    returned = lax.all_to_all(answers, "seq", split_axis=0, concat_axis=0, tiled=True)
    picked = returned.reshape(seq_count * slots, BLOCK, 2, feat_dev)[slot]
    return picked.reshape(blocks_dev, entries // blocks_dev * BLOCK, 2, feat_dev)


def body(queries, keys_values, rand_blocks, w_out):
    tok_rows, feat_dev = queries.shape
    heads_dev = feat_dev // HEAD_DIM
    blocks_dev = tok_rows // BLOCK
    seq_count = lax.axis_size("seq")
    all_blocks = blocks_dev * seq_count
    position = lax.axis_index("seq")
    scale = HEAD_DIM ** (-0.5)
    padded = with_halo(keys_values, (("seq", 0),), BLOCK)
    padded = padded.reshape(blocks_dev + 2, BLOCK, 2, heads_dev, HEAD_DIM)
    window = jnp.concatenate([padded[:-2], padded[1:-1], padded[2:]], axis=1)
    first = spread(keys_values[:BLOCK], "seq", 0)
    final = spread(keys_values[-BLOCK:], "seq", seq_count - 1)
    ends = jnp.concatenate([first, final], axis=0)
    ends = ends.reshape(2 * BLOCK, 2, heads_dev, HEAD_DIM)
    random_kv = fetch_random(keys_values, rand_blocks, blocks_dev, seq_count)
    random_kv = random_kv.reshape(blocks_dev, -1, 2, heads_dev, HEAD_DIM)
    block_ids = position * blocks_dev + jnp.arange(blocks_dev, dtype=jnp.int32)
    near_ok = jnp.stack([block_ids >= 1, block_ids >= 0, block_ids <= all_blocks - 2], axis=1)
    ends_ok = jnp.stack([block_ids >= 2, block_ids <= all_blocks - 3], axis=1)
    taken = [
        block_ids - 1,
        block_ids,
        block_ids + 1,
        jnp.zeros_like(block_ids),
        jnp.zeros_like(block_ids) + (all_blocks - 1),
    ]
    rand_flags = []
    for column in range(rand_blocks.shape[1]):
        chosen = rand_blocks[:, column]
        clash = reduce(jnp.logical_or, [chosen == other for other in taken])
        rand_flags.append(jnp.logical_not(clash))
        taken.append(chosen)
    rand_ok = jnp.stack(rand_flags, axis=1)
    near_mask = jnp.repeat(near_ok, BLOCK, axis=1)[:, None, None, :]
    ends_mask = jnp.repeat(ends_ok, BLOCK, axis=1)[:, None, None, :]
    rand_mask = jnp.repeat(rand_ok, BLOCK, axis=1)[:, None, None, :]
    query_heads = queries.reshape(blocks_dev, BLOCK, heads_dev, HEAD_DIM)
    near_scores = (
        jnp.einsum(
            "jqhd,jkhd->jhqk", query_heads, window[:, :, 0], preferred_element_type=jnp.float32
        )
        * scale
    )
    ends_scores = (
        jnp.einsum("jqhd,khd->jhqk", query_heads, ends[:, 0], preferred_element_type=jnp.float32)
        * scale
    )
    rand_scores = (
        jnp.einsum(
            "jqhd,jkhd->jhqk", query_heads, random_kv[:, :, 0], preferred_element_type=jnp.float32
        )
        * scale
    )
    near_scores = jnp.where(near_mask, near_scores, -1e30)
    ends_scores = jnp.where(ends_mask, ends_scores, -1e30)
    rand_scores = jnp.where(rand_mask, rand_scores, -1e30)
    peak = jnp.maximum(
        jnp.max(near_scores, axis=-1, keepdims=True), jnp.max(ends_scores, axis=-1, keepdims=True)
    )
    peak = jnp.maximum(peak, jnp.max(rand_scores, axis=-1, keepdims=True))
    near_raw = jnp.where(near_mask, jnp.exp(near_scores - peak), 0.0)
    ends_raw = jnp.where(ends_mask, jnp.exp(ends_scores - peak), 0.0)
    rand_raw = jnp.where(rand_mask, jnp.exp(rand_scores - peak), 0.0)
    total = jnp.sum(near_raw, axis=-1) + jnp.sum(ends_raw, axis=-1) + jnp.sum(rand_raw, axis=-1)
    mixture = jnp.einsum(
        "jhqk,jkhd->jqhd",
        near_raw.astype(jnp.bfloat16),
        window[:, :, 1],
        preferred_element_type=jnp.float32,
    )
    mixture = mixture + jnp.einsum(
        "jhqk,khd->jqhd",
        ends_raw.astype(jnp.bfloat16),
        ends[:, 1],
        preferred_element_type=jnp.float32,
    )
    mixture = mixture + jnp.einsum(
        "jhqk,jkhd->jqhd",
        rand_raw.astype(jnp.bfloat16),
        random_kv[:, :, 1],
        preferred_element_type=jnp.float32,
    )
    attended = (mixture / jnp.transpose(total, (0, 2, 1))[..., None]).astype(jnp.bfloat16)
    attended = attended.reshape(tok_rows, feat_dev)
    return lax.psum_scatter(
        jnp.dot(attended, w_out, preferred_element_type=jnp.float32).astype(jnp.bfloat16),
        "head",
        scatter_dimension=0,
        tiled=True,
    )


def solution(mesh):
    in_specs = (P("seq", "head"), P("seq", None, "head"), P("seq", None), P("head", None))
    out_specs = P(("seq", "head"), None)
    return jax.shard_map(body, mesh=mesh, in_specs=in_specs, out_specs=out_specs, check_vma=False)
```

profile of v0, /device:TPU:0, one launch (start us, length us, event | category | flops | bytes accessed | tf_op | source)
XLA Modules:
  0.0 300.0 jit_solution(7873285901964880641)
XLA Ops:
  6.5 0.8 copy.201
  7.4 0.2 convert_reduce_fusion
  7.8 13.5 %all_to_all.17 = s32[8,1,4]{2,1,0:T(1,128)S(1)} all-to-all(s32[8,1,4]{2,1,0:T(1,128)S(1)} %bitcast.118), channel_id=1, replica_groups=mesh['seq'=8,'head'=4] {'seq'}, dimensions={0} | all-to-all | bytes 256 | tf_op jit(solution)/shard_map/all_to_all | solution.py:46
  21.6 11.7 %gather_fusion = bf16[32,64,2,512]{3,2,1,0:T(2,128)(2,1)} fusion(bf16[16,64,2,512]{3,2,1,0:T(2,128)(2,1)} %bitcast.108, s32[1024]{0:T(1024)S(1)} %pad_clamp_fusion.1), kind=kCustom, calls=%fused_computation | custom fusion | bytes 8388736 | tf_op jit(solution)/shard_map/gather | solution.py:50
  33.3 5.3 %copy.205 = bf16[32,64,2,512]{3,1,2,0:T(8,128)(2,1)} copy(bf16[32,64,2,512]{3,2,1,0:T(2,128)(2,1)} %gather_fusion) | data formatting | bytes 8388608 | tf_op jit(solution)/shard_map/gather | solution.py:50
  38.6 4.7 %all-to-all-start.1 = ((bf16[8,4,64,2,512]{4,2,3,1,0:T(8,128)(2,1)}), bf16[8,4,64,2,512]{4,2,3,1,0:T(8,128)(2,1)}, u32[]{:S(2)}, u32[]{:S(2)}) async-start(bf16[8,4,64,2,512]{4,2,3,1,0:T(8,128)(2,1)} %bitcast.111), calls=%async_computation.1 | async-start | bytes 8388608 | tf_op jit(solution)/shard_map/all_to_all | solution.py:51
  43.4 0.2 fusion.52
  43.5 0.2 copy.229
  43.7 4.5 %collective-permute-start = (bf16[64,2,512]{0,2,1:T(8,128)(2,1)S(1)}, bf16[64,2,512]{0,2,1:T(8,128)(2,1)}, u32[]{:S(2)}, u32[]{:S(2)}) collective-permute-start(bf16[64,2,512]{0,2,1:T(8,128)(2,1)S(1)} %copy.229), channel_id=1, source_target_pairs={{0,4},{4,8},{8,12},{12,16},{16,20},{20,24},{24,28},{1,5},{5,9},{9,... | collective-permute-start | bytes 393224 | tf_op jit(solution)/shard_map/ppermute | solution.py:20
  48.2 0.9 copy.230
  49.1 1.3 collective-permute-start.1
  50.4 0.7 broadcast_select_fusion
  51.1 1.7 broadcast_select_fusion.1
  52.8 0.2 reduce-scatter.2.cloned.1.call-start
  53.2 2.6 reshape.290
  55.8 1.1 reshape.262
  57.0 1.5 copy.198
  58.4 0.1 copy.196
  59.3 26.7 %collective-permute-done = bf16[64,2,512]{0,2,1:T(8,128)(2,1)} collective-permute-done((bf16[64,2,512]{0,2,1:T(8,128)(2,1)S(1)}, bf16[64,2,512]{0,2,1:T(8,128)(2,1)}, u32[]{:S(2)}, u32[]{:S(2)}) %collective-permute-start) | collective-permute-done | bytes 131104 | tf_op jit(solution)/shard_map/ppermute | solution.py:20
  86.0 1.1 copy.185
  87.1 1.1 copy.189
  88.2 6.5 %pad_maximum_fusion = (bf16[1024,2,512]{2,1,0:T(2,128)(2,1)}, bf16[1024,2,512]{2,1,0:T(2,128)(2,1)}) fusion(bf16[64,2,512]{2,1,0:T(2,128)(2,1)S(1)} %copy.189, bf16[1024,2,512]{2,1,0:T(2,128)(2,1)S(1)} %copy-done, bf16[64,2,512]{2,1,0:T(2,128)(2,1)S(1)} %copy.185), kind=kLoop, calls=%fused_computation.14 | loop fusion | flops 2097152 | bytes 6553600 | tf_op jit(solution)/shard_map/concatenate | solution.py:18
  94.7 4.5 %reshape.289 = bf16[16,64,2,4,128]{4,3,2,1,0:T(4,128)(2,1)} reshape(bf16[1024,2,512]{2,1,0:T(2,128)(2,1)} %get-tuple-element.13) | data formatting | bytes 4194304 | tf_op jit(solution)/shard_map/slice | solution.py:66
  99.3 2.6 reshape.291
  101.9 2.3 copy_dynamic-update-slice_fusion.2
  104.2 0.7 copy_dynamic-update-slice_fusion.1
  104.9 0.9 copy-done.3
  105.8 0.7 copy_dynamic-update-slice_fusion
  106.5 2.6 copy-done.8
  109.2 4.1 %bitcast_reduce_fusion = (f32[16,4,64]{2,1,0:T(4,128)S(1)}, f32[16,4,192,64]{2,3,1,0:T(8,128)}) fusion(pred[16,192]{1,0:T(8,128)(4,1)S(1)} %broadcast_in_dim.93, bf16[16,64,4,128]{3,2,1,0:T(4,128)(2,1)S(1)} %copy-done.5, bf16[16,192,2,4,128]{4,1,3,0,2:T(8,128)(2,1)S(1)} %copy_dynamic-update-slice_fusion), kind=kOutput, calls=%fused_computation.4 | convolution fusion | flops 203681792 | bytes 7360512 | tf_op jit(solution)/shard_map/jqhd,jkhd->jhqk/dot_general | solution.py:95
  113.3 68.9 %all-reduce.3.cloned.1.call-done = (bf16[64,2,512]{0,2,1:T(8,128)(2,1)}, bf16[64,2,512]{0,2,1:T(8,128)(2,1)}) async-done(((bf16[64,2,512]{0,2,1:T(8,128)(2,1)}, bf16[64,2,512]{0,2,1:T(8,128)(2,1)}), (bf16[64,2,512]{0,2,1:T(8,128)(2,1)}, bf16[64,2,512]{0,2,1:T(8,128)(2,1)})) %all-reduce.3.cloned.1.call-update) | async-done | bytes 262160 | tf_op jit(solution)/shard_map/psum | solution.py:31
  182.2 1.2 pad_maximum_fusion.2
  183.4 0.4 fusion.34
  183.8 0.6 fusion.21
  184.4 5.1 %gather_fusion.1 = bf16[32,64,2,512]{3,1,2,0:T(8,128)(2,1)} fusion(bf16[32,64,2,512]{3,1,2,0:T(8,128)(2,1)} %bitcast.13, s32[1024]{0:T(1024)S(1)} %pad_clamp_fusion), kind=kCustom, calls=%fused_computation.1 | custom fusion | bytes 8388736 | tf_op jit(solution)/shard_map/gather | solution.py:52
  189.5 4.7 %copy.207 = bf16[32,64,2,512]{3,1,0,2:T(8,128)(2,1)} copy(bf16[32,64,2,512]{3,1,2,0:T(8,128)(2,1)} %gather_fusion.1) | data formatting | bytes 8388608 | tf_op jit(solution)/shard_map/gather | solution.py:52
  194.2 6.9 %reshape_reshape.3 = bf16[16,128,2,4,128]{4,3,1,0,2:T(4,128)(2,1)} reshape(bf16[32,64,2,512]{3,1,0,2:T(8,128)(2,1)} %copy.207) | data formatting | bytes 8388608 | tf_op jit(solution)/shard_map/reshape;reshape | solution.py:72
  201.1 3.2 %fusion.51 = (bf16[16,128,1,4,128]{4,3,1,0,2:T(4,128)(2,1)S(1)}, bf16[16,128,1,4,128]{4,3,1,0,2:T(4,128)(2,1)S(1)}) fusion(bf16[16,128,2,4,128]{4,3,1,0,2:T(4,128)(2,1)} %reshape_reshape.3), kind=kLoop, calls=%fused_computation.101 | loop fusion | bytes 8388608 | tf_op jit(solution)/shard_map/slice | solution.py:106
  204.3 1.6 bitcast_reduce_fusion.1
  206.0 2.7 fusion.22
  208.8 1.9 fusion.4
  210.7 0.4 fusion.29
  211.1 0.7 fusion.10
  211.8 0.5 slice-done.1
  212.3 2.2 fusion.12
  214.5 0.9 copy.218
  215.4 6.7 %convolution_convert_fusion = bf16[1024,4096]{1,0:T(8,128)(2,1)} fusion(bf16[512,4096]{1,0:T(8,128)(2,1)S(1)} %copy-done.10, bf16[128,8,4,128]{3,2,1,0:T(4,128)(2,1)S(1)} %bitcast.115), kind=kOutput, calls=%fused_computation.2 | convolution fusion | flops 4299161600 | bytes 13631488 | tf_op jit(solution)/shard_map/dot_general | solution.py:142
  222.1 71.1 %reduce-scatter.2.cloned.1.call-done = bf16[256,4096]{1,0:T(8,128)(2,1)} async-done(((bf16[1024,4096]{1,0:T(8,128)(2,1)}), bf16[256,4096]{1,0:T(8,128)(2,1)}) %reduce-scatter.2.cloned.1.call-update) | async-done | bytes 2097168 | tf_op jit(solution)/shard_map/reduce_scatter | solution.py:141
  (60 shorter events, 1.6 us)
Async XLA Ops:
  38.6 4.8 %copy-start = (bf16[1024,2,512]{2,1,0:T(2,128)(2,1)S(1)}, bf16[1024,2,512]{2,1,0:T(2,128)(2,1)}, u32[]{:S(2)}) copy-start(bf16[1024,2,512]{2,1,0:T(2,128)(2,1)} %param.5) | copy-start | bytes 6291460
  38.6 145.8 %all-to-all-start.1 = ((bf16[8,4,64,2,512]{4,2,3,1,0:T(8,128)(2,1)}), bf16[8,4,64,2,512]{4,2,3,1,0:T(8,128)(2,1)}, u32[]{:S(2)}, u32[]{:S(2)}) async-start(bf16[8,4,64,2,512]{4,2,3,1,0:T(8,128)(2,1)} %bitcast.111), calls=%async_computation.1 | async-start | bytes 8388608 | tf_op jit(solution)/shard_map/all_to_all | solution.py:51
  43.3 9.8 %copy-start.9 = (s32[16,2]{0,1:T(2,128)S(1)}, s32[16,2]{0,1:T(2,128)}, u32[]{:S(2)}) copy-start(s32[16,2]{0,1:T(2,128)} %param.6) | copy-start | bytes 388
  43.3 138.9 %all-reduce.3.cloned.1.call-start = ((), (), s32[]{:S(2)}) async-start(), calls=%async_computation.4 | async-start | bytes 1048576 | tf_op jit(solution)/shard_map/psum | solution.py:31
  43.7 42.3 %collective-permute-start = (bf16[64,2,512]{0,2,1:T(8,128)(2,1)S(1)}, bf16[64,2,512]{0,2,1:T(8,128)(2,1)}, u32[]{:S(2)}, u32[]{:S(2)}) collective-permute-start(bf16[64,2,512]{0,2,1:T(8,128)(2,1)S(1)} %copy.229), channel_id=1, source_target_pairs={{0,4},{4,8},{8,12},{12,16},{16,20},{20,24},{24,28},{1,5},{5,9},{9,... | collective-permute-start | bytes 393224 | tf_op jit(solution)/shard_map/ppermute | solution.py:20
  49.1 38.0 %collective-permute-start.1 = (bf16[64,2,512]{0,2,1:T(8,128)(2,1)}, bf16[64,2,512]{0,2,1:T(8,128)(2,1)}, u32[]{:S(2)}, u32[]{:S(2)}) collective-permute-start(bf16[64,2,512]{0,2,1:T(8,128)(2,1)} %copy.230), channel_id=1, source_target_pairs={{4,0},{8,4},{12,8},{16,12},{20,16},{24,20},{28,24},{5,1},{9,5},{13... | collective-permute-start | bytes 393224 | tf_op jit(solution)/shard_map/ppermute | solution.py:22
  52.8 240.4 %reduce-scatter.2.cloned.1.call-start = ((), (), s32[]{:S(2)}) async-start(), calls=%async_computation.3 | async-start | bytes 10485760 | tf_op jit(solution)/shard_map/reduce_scatter | solution.py:141
  53.2 2.6 copy-start.7
  94.7 4.5 %copy-start.1 = (bf16[1024,2,512]{2,1,0:T(2,128)(2,1)S(1)}, bf16[1024,2,512]{2,1,0:T(2,128)(2,1)}, u32[]{:S(2)}) copy-start(bf16[1024,2,512]{2,1,0:T(2,128)(2,1)} %get-tuple-element.12) | copy-start | bytes 6291460
  101.8 2.3 copy-start.2
  104.2 1.6 copy-start.3
  105.8 3.4 %copy-start.5 = (bf16[16,64,4,128]{3,2,1,0:T(4,128)(2,1)S(1)}, bf16[16,64,4,128]{3,2,1,0:T(4,128)(2,1)}, u32[]{:S(2)}) copy-start(bf16[16,64,4,128]{3,2,1,0:T(4,128)(2,1)} %reshape.262) | copy-start | bytes 3145732
  106.5 2.7 copy-start.8
  201.1 3.2 %copy-start.6 = (bf16[16,64,4,128]{3,2,1,0:T(4,128)(2,1)S(1)}, bf16[16,64,4,128]{3,2,1,0:T(4,128)(2,1)}, u32[]{:S(2)}) copy-start(bf16[16,64,4,128]{3,2,1,0:T(4,128)(2,1)} %reshape.262) | copy-start | bytes 3145732
  206.0 2.8 copy-start.4
  208.8 3.0 %slice-start = ((s8[6291456]{0:T(1024)(128)(4,1)}), s8[4194304]{0:T(1024)(128)(4,1)S(1)}, s32[]{:S(2)}) async-start(s8[6291456]{0:T(1024)(128)(4,1)} %bitcast.116), calls=%async_computation.5 | async-start | bytes 8388608
  210.7 1.7 slice-start.1
  212.3 3.1 %copy-start.10 = (bf16[512,4096]{1,0:T(8,128)(2,1)S(1)}, bf16[512,4096]{1,0:T(8,128)(2,1)}, u32[]{:S(2)}) copy-start(bf16[512,4096]{1,0:T(8,128)(2,1)} %param.7) | copy-start | bytes 12582916
Sparse Core Ops, SparseCore 0:
  52.9 129.2 all-reduce.2
  222.3 70.8 reduce-scatter.1
where the time goes:
time: 301 us; the launch traced here: 300 us
  waiting for transfers between devices  167 us (55%)
  local copies, waits for them, and re-layouts  63.4 us (21%)
  matrix products  16.1 us (5%)
  other arithmetic  15.7 us (5%)
  between operations  13.8 us (5%)
  blocking collectives  13.5 us (4%)
  starting transfers between devices  10.7 us (4%)
    reduce_scatter x1, waiting for transfers between devices, body(): lax.psum_scatter(jnp.dot(attended, w_out, preferred_element_type=jnp.floa...  71.1 us
    psum x1, waiting for transfers between devices, spread(): return lax.psum(jnp.where(mine, array, jnp.zeros_like(array)), axis)  68.9 us
    ppermute x1, waiting for transfers between devices, with_halo(): lax.ppermute(tail, axis, [(i, (i + 1) % count) for i in range(ends)])  26.7 us
    gather x2, local copies, waits for them, and re-layouts, fetch_random(): answers = local_blocks[wanted]  17 us
    all_to_all x1, blocking collectives, fetch_random(): lax.all_to_all(outgoing.reshape(seq_count, slots), 'seq', split_axis=0, c...  13.5 us
    gather x2, local copies, waits for them, and re-layouts, fetch_random(): picked = returned.reshape(seq_count * slots, BLOCK, 2, feat_dev)[slot]  9.76 us
    slice x3, local copies, waits for them, and re-layouts, body(): window = jnp.concatenate([padded[:-2], padded[1:-1], padded[2:]], axis=1)  9.72 us
    unnamed x31, local copies, waits for them, and re-layouts  8.94 us
  transfers between devices with their start and end apart: 5, of which 3 were waited for; matrix products, arithmetic and copies ran while one was open for 12% of the time, Pallas kernels for 0%

commit v1 on v0

v1 whole, which is shorter than its diff:
```python
import functools
from functools import reduce

import jax
import jax.numpy as jnp
from jax import lax
from jax.experimental import pallas as pl
from jax.experimental.pallas import tpu as pltpu
from jax.sharding import PartitionSpec as P

HEAD_DIM = 128
BLOCK = 64
W_CHUNKS = 4
NEG = -1e30


def kernel(
    n,
    slots,
    blocks,
    heads,
    q_ref,
    kv_ref,
    tab_ref,
    slot_ref,
    bias_ref,
    w_ref,
    out_ref,
    kvp,
    ends,
    tabs,
    tabs_s,
    stage,
    recv,
    m_ref,
    l_ref,
    acc,
    att,
    attr,
    wall,
    oacc,
    tab_send,
    tab_recv,
    tab_local,
    halo_send,
    halo_recv,
    first_send,
    final_send,
    ends_recv,
    rand_send,
    rand_recv,
    w_local,
    wx_send,
    wx_recv,
    ws_send,
    ws_recv,
    wf_send,
    wf_recv,
    att_send,
    att_recv,
):
    me = lax.axis_index("seq")
    h = lax.axis_index("head")
    sib = h + 1 - 2 * lax.rem(h, 2)
    across = lax.rem(h + 2, 4)
    across_sib = lax.rem(sib + 2, 4)
    others = (across, across_sib, sib)
    total_blocks = n * blocks
    scale = HEAD_DIM ** (-0.5)
    w_rows = w_ref.shape[0] // W_CHUNKS
    feat = heads * HEAD_DIM

    def remote(src, dst, ssem, rsem, seq, head):
        return pltpu.make_async_remote_copy(
            src_ref=src,
            dst_ref=dst,
            send_sem=ssem,
            recv_sem=rsem,
            device_id=(seq, head),
            device_id_type=pl.DeviceIdType.MESH,
        )

    def peer(i):
        step = (i + 1) // 2
        d = n // 2 + step * (2 * lax.rem(i, 2) - 1)
        return lax.rem(me + d, n)

    barrier = pltpu.get_barrier_semaphore()

    def greet(i, c):
        pl.semaphore_signal(
            barrier, inc=1, device_id=(peer(i), h), device_id_type=pl.DeviceIdType.MESH
        )
        return c

    lax.fori_loop(0, n - 1, greet, 0)
    for g in others:
        pl.semaphore_signal(barrier, inc=1, device_id=(me, g), device_id_type=pl.DeviceIdType.MESH)
    pl.semaphore_wait(barrier, n - 1 + 3)

    def tab_copy(s, dest):
        return remote(
            tab_ref, tabs.at[pl.ds(s * 8, 8)], tab_send.at[dest], tab_recv.at[s], dest, h
        )

    def tab_start(i, c):
        tab_copy(me, peer(i)).start()
        return c

    lax.fori_loop(0, n - 1, tab_start, 0)

    def to_right():
        return remote(
            kv_ref.at[blocks - 1], kvp.at[0], halo_send.at[0], halo_recv.at[0], lax.rem(me + 1, n), h
        )

    def to_left():
        return remote(
            kv_ref.at[0],
            kvp.at[blocks + 1],
            halo_send.at[1],
            halo_recv.at[1],
            lax.rem(me + n - 1, n),
            h,
        )

    def first_copy(dest):
        return remote(kv_ref.at[0], ends.at[0], first_send.at[dest], ends_recv.at[0], dest, h)

    def final_copy(dest):
        return remote(kv_ref.at[blocks - 1], ends.at[1], final_send.at[dest], ends_recv.at[1], dest, h)

    @pl.when(me == 0)
    def _():
        def go(i, c):
            first_copy(peer(i)).start()
            return c

        lax.fori_loop(0, n - 1, go, 0)
        ends[0] = kv_ref[0]
        kvp[0] = jnp.zeros_like(kvp[0])

    @pl.when(me == n - 1)
    def _():
        def go(i, c):
            final_copy(peer(i)).start()
            return c

        lax.fori_loop(0, n - 1, go, 0)
        ends[1] = kv_ref[blocks - 1]
        kvp[blocks + 1] = jnp.zeros_like(kvp[0])

    @pl.when(me < n - 1)
    def _():
        to_right().start()

    @pl.when(me > 0)
    def _():
        to_left().start()

    def w_piece(g, c):
        return wall.at[g, pl.ds(c * w_rows, w_rows)]

    def wx_copy(g, c):
        return remote(
            w_ref.at[pl.ds(c * w_rows, w_rows)],
            w_piece(g, c),
            wx_send.at[c],
            wx_recv.at[c],
            me,
            across,
        )

    for c in range(W_CHUNKS):
        wx_copy(h, c).start()

    def tab_wait(i, c):
        tab_copy(peer(i), me).wait_recv()
        return c

    lax.fori_loop(0, n - 1, tab_wait, 0)
    tabs[pl.ds(pl.multiple_of(me * 8, 8), 8), :] = tab_ref[...]
    to_smem = pltpu.make_async_copy(tabs, tabs_s, tab_local)
    to_smem.start()
    to_smem.wait()

    def rand_copy(s, dest):
        return remote(stage.at[dest], recv.at[s], rand_send.at[dest], rand_recv.at[s], dest, h)

    def rand_start(i, c):
        dest = peer(i)
        for k in range(slots):
            stage[dest, k] = kv_ref[tabs_s[dest * 8, me * slots + k]]
        rand_copy(me, dest).start()
        return c

    lax.fori_loop(0, n - 1, rand_start, 0)
    for k in range(slots):
        recv[me, k] = kv_ref[tabs_s[me * 8, me * slots + k]]

    w_own = pltpu.make_async_copy(w_ref, wall.at[h], w_local)
    w_own.start()
    ws_copy = remote(w_ref, wall.at[h], ws_send, ws_recv, me, sib)
    ws_copy.start()

    def fill(j, c):
        kvp[j + 1] = kv_ref[j]
        return c

    lax.fori_loop(0, blocks, fill, 0)

    @pl.when(me > 0)
    def _():
        to_right().wait_recv()
        first_copy(me).wait_recv()

    @pl.when(me < n - 1)
    def _():
        to_left().wait_recv()
        final_copy(me).wait_recv()

    nt = (((1,), (1,)), ((), ()))

    def near(j, c):
        block = me * blocks + j
        rows = pl.ds(pl.multiple_of(j * BLOCK, BLOCK), BLOCK)
        b_prev = jnp.where(block >= 1, 0.0, NEG)
        b_next = jnp.where(block <= total_blocks - 2, 0.0, NEG)
        b_first = jnp.where(block >= 2, 0.0, NEG)
        b_final = jnp.where(block <= total_blocks - 3, 0.0, NEG)
        col = lax.broadcasted_iota(jnp.int32, (BLOCK, 3 * BLOCK), 1)
        b_win = jnp.where(col < BLOCK, b_prev, jnp.where(col >= 2 * BLOCK, b_next, 0.0))
        cole = lax.broadcasted_iota(jnp.int32, (BLOCK, 2 * BLOCK), 1)
        b_end = jnp.where(cole < BLOCK, b_first, b_final)
        for hd in range(heads):
            kc = pl.ds(hd * HEAD_DIM, HEAD_DIM)
            vc = pl.ds(feat + hd * HEAD_DIM, HEAD_DIM)
            qh = q_ref[rows, kc]
            kw = kvp[pl.ds(j, 3), :, kc].reshape(3 * BLOCK, HEAD_DIM)
            vw = kvp[pl.ds(j, 3), :, vc].reshape(3 * BLOCK, HEAD_DIM)
            ke = ends[:, :, kc].reshape(2 * BLOCK, HEAD_DIM)
            ve = ends[:, :, vc].reshape(2 * BLOCK, HEAD_DIM)
            sw = lax.dot_general(qh, kw, nt, preferred_element_type=jnp.float32) * scale + b_win
            se = lax.dot_general(qh, ke, nt, preferred_element_type=jnp.float32) * scale + b_end
            m = jnp.maximum(
                jnp.max(sw, axis=1, keepdims=True), jnp.max(se, axis=1, keepdims=True)
            )
            pw = jnp.exp(sw - m)
            pe = jnp.exp(se - m)
            tot = jnp.sum(pw, axis=1, keepdims=True) + jnp.sum(pe, axis=1, keepdims=True)
            o = jnp.dot(pw.astype(jnp.bfloat16), vw, preferred_element_type=jnp.float32)
            o = o + jnp.dot(pe.astype(jnp.bfloat16), ve, preferred_element_type=jnp.float32)
            m_ref[rows, kc] = jnp.broadcast_to(m, (BLOCK, HEAD_DIM))
            l_ref[rows, kc] = jnp.broadcast_to(tot, (BLOCK, HEAD_DIM))
            acc[rows, kc] = o
        return c

    lax.fori_loop(0, blocks, near, 0)

    def wf_copy(g, c):
        return remote(w_piece(g, c), w_piece(g, c), wf_send.at[c], wf_recv.at[c], me, sib)

    def forward(c):
        wx_copy(across, c).wait_recv()
        wf_copy(across, c).start()

    for c in range(W_CHUNKS - 1):
        forward(c)

    def rand_wait(i, c):
        rand_copy(peer(i), me).wait_recv()
        return c

    lax.fori_loop(0, n - 1, rand_wait, 0)

    quarter = blocks // 4

    def far(t):
        def one(u, c):
            j = t * quarter + u
            rows = pl.ds(pl.multiple_of(j * BLOCK, BLOCK), BLOCK)
            urows = pl.ds(pl.multiple_of(u * BLOCK, BLOCK), BLOCK)
            s0 = slot_ref[2 * j]
            s1 = slot_ref[2 * j + 1]
            col = lax.broadcasted_iota(jnp.int32, (BLOCK, 2 * BLOCK), 1)
            bias = jnp.where(col < BLOCK, bias_ref[2 * j], bias_ref[2 * j + 1])
            r0, k0 = s0 // slots, lax.rem(s0, slots)
            r1, k1 = s1 // slots, lax.rem(s1, slots)
            for hd in range(heads):
                kc = pl.ds(hd * HEAD_DIM, HEAD_DIM)
                vc = pl.ds(feat + hd * HEAD_DIM, HEAD_DIM)
                keys = jnp.concatenate([recv[r0, k0, :, kc], recv[r1, k1, :, kc]], axis=0)
                vals = jnp.concatenate([recv[r0, k0, :, vc], recv[r1, k1, :, vc]], axis=0)
                s = lax.dot_general(q_ref[rows, kc], keys, nt, preferred_element_type=jnp.float32)
                s = s * scale + bias
                m0 = m_ref[rows, kc]
                m = jnp.maximum(m0, jnp.max(s, axis=1, keepdims=True))
                alpha = jnp.exp(m0 - m)
                p = jnp.exp(s - m)
                tot = l_ref[rows, kc] * alpha + jnp.sum(p, axis=1, keepdims=True)
                o = jnp.dot(p.astype(jnp.bfloat16), vals, preferred_element_type=jnp.float32)
                o = o + acc[rows, kc] * alpha
                att[t, urows, kc] = (o / tot).astype(jnp.bfloat16)
            return c

        lax.fori_loop(0, quarter, one, 0)

    def att_copy(t, g):
        return remote(att.at[t], attr.at[g], att_send.at[t], att_recv.at[g], me, t)

    for t in others:
        far(t)
        att_copy(t, h).start()
    far(h)

    forward(W_CHUNKS - 1)
    w_own.wait()
    ws_copy.wait_recv()
    att_copy(h, sib).wait_recv()

    tile = 512
    tiles = out_ref.shape[1] // tile

    def project_a(i, c):
        cols = pl.ds(pl.multiple_of(i * tile, tile), tile)
        o = jnp.dot(att[h], wall[h, :, cols], preferred_element_type=jnp.float32)
        o = o + jnp.dot(attr[sib], wall[sib, :, cols], preferred_element_type=jnp.float32)
        oacc[:, cols] = o
        return c

    lax.fori_loop(0, tiles, project_a, 0)
    for c in range(W_CHUNKS):
        wf_copy(across_sib, c).wait_recv()
    att_copy(h, across).wait_recv()
    att_copy(h, across_sib).wait_recv()

    def project_b(i, c):
        cols = pl.ds(pl.multiple_of(i * tile, tile), tile)
        o = oacc[:, cols]
        o = o + jnp.dot(attr[across], wall[across, :, cols], preferred_element_type=jnp.float32)
        o = o + jnp.dot(
            attr[across_sib], wall[across_sib, :, cols], preferred_element_type=jnp.float32
        )
        out_ref[:, cols] = o.astype(jnp.bfloat16)
        return c

    lax.fori_loop(0, tiles, project_b, 0)

    def drain(i, c):
        tab_copy(me, peer(i)).wait_send()
        rand_copy(me, peer(i)).wait_send()
        return c

    lax.fori_loop(0, n - 1, drain, 0)

    @pl.when(me == 0)
    def _():
        def go(i, c):
            first_copy(peer(i)).wait_send()
            return c

        lax.fori_loop(0, n - 1, go, 0)

    @pl.when(me == n - 1)
    def _():
        def go(i, c):
            final_copy(peer(i)).wait_send()
            return c

        lax.fori_loop(0, n - 1, go, 0)

    @pl.when(me < n - 1)
    def _():
        to_right().wait_send()

    @pl.when(me > 0)
    def _():
        to_left().wait_send()

    for c in range(W_CHUNKS):
        wx_copy(h, c).wait_send()
        wf_copy(across, c).wait_send()
    ws_copy.wait_send()
    for t in others:
        att_copy(t, h).wait_send()


def body(queries, keys_values, rand_blocks, w_out):
    tok_rows, feat = queries.shape
    heads = feat // HEAD_DIM
    blocks = tok_rows // BLOCK
    n = lax.axis_size("seq")
    n_head = lax.axis_size("head")
    all_blocks = blocks * n
    position = lax.axis_index("seq")
    entries = rand_blocks.shape[0] * rand_blocks.shape[1]
    slots = max(1, entries // n)
    width = w_out.shape[1]

    flat = rand_blocks.reshape(entries)
    owner = flat // blocks
    offset = flat % blocks
    earlier = jnp.arange(entries)[:, None] > jnp.arange(entries)[None, :]
    rank = jnp.sum((owner[:, None] == owner[None, :]) & earlier, axis=1)
    slot = (owner * slots + rank).astype(jnp.int32)
    placed = slot[:, None] == jnp.arange(128)[None, :]
    outgoing = jnp.sum(jnp.where(placed, offset[:, None], 0), axis=0).astype(jnp.int32)
    table = jnp.broadcast_to(outgoing[None, :], (8, 128))

    ids = position * blocks + jnp.arange(blocks, dtype=jnp.int32)
    taken = [ids - 1, ids, ids + 1, jnp.zeros_like(ids), jnp.zeros_like(ids) + (all_blocks - 1)]
    flags = []
    for column in range(rand_blocks.shape[1]):
        chosen = rand_blocks[:, column]
        flags.append(reduce(jnp.logical_or, [chosen == other for other in taken]))
        taken.append(chosen)
    bias = jnp.where(jnp.stack(flags, axis=1), NEG, 0.0).astype(jnp.float32).reshape(entries)

    kv = keys_values.reshape(blocks, BLOCK, 2 * feat)
    vmem = pl.BlockSpec(memory_space=pltpu.VMEM)
    smem = pl.BlockSpec(memory_space=pltpu.SMEM)
    bf16, f32, i32 = jnp.bfloat16, jnp.float32, jnp.int32
    rows_out = tok_rows // n_head
    dma = pltpu.SemaphoreType.DMA
    return pl.pallas_call(
        functools.partial(kernel, n, slots, blocks, heads),
        out_shape=jax.ShapeDtypeStruct((rows_out, width), bf16),
        in_specs=[vmem, vmem, vmem, smem, smem, pl.BlockSpec(memory_space=pl.ANY)],
        out_specs=vmem,
        scratch_shapes=[
            pltpu.VMEM((blocks + 2, BLOCK, 2 * feat), bf16),
            pltpu.VMEM((2, BLOCK, 2 * feat), bf16),
            pltpu.VMEM((n * 8, 128), i32),
            pltpu.SMEM((n * 8, 128), i32),
            pltpu.VMEM((n, slots, BLOCK, 2 * feat), bf16),
            pltpu.VMEM((n, slots, BLOCK, 2 * feat), bf16),
            pltpu.VMEM((tok_rows, feat), f32),
            pltpu.VMEM((tok_rows, feat), f32),
            pltpu.VMEM((tok_rows, feat), f32),
            pltpu.VMEM((n_head, rows_out, feat), bf16),
            pltpu.VMEM((n_head, rows_out, feat), bf16),
            pltpu.VMEM((n_head, feat, width), bf16),
            pltpu.VMEM((rows_out, width), f32),
            dma((n,)),
            dma((n,)),
            dma,
            dma((2,)),
            dma((2,)),
            dma((n,)),
            dma((n,)),
            dma((2,)),
            dma((n,)),
            dma((n,)),
            dma,
            dma((W_CHUNKS,)),
            dma((W_CHUNKS,)),
            dma,
            dma,
            dma((W_CHUNKS,)),
            dma((W_CHUNKS,)),
            dma((n_head,)),
            dma((n_head,)),
        ],
        compiler_params=pltpu.CompilerParams(
            collective_id=0, has_side_effects=True, vmem_limit_bytes=60 * 1024 * 1024
        ),
        cost_estimate=pl.CostEstimate(
            flops=6_000_000_000, bytes_accessed=20_000_000, transcendentals=2_000_000
        ),
    )(queries, kv, table, slot, bias, w_out)


def solution(mesh):
    in_specs = (P("seq", "head"), P("seq", None, "head"), P("seq", None), P("head", None))
    out_specs = P(("seq", "head"), None)
    return jax.shard_map(body, mesh=mesh, in_specs=in_specs, out_specs=out_specs, check_vma=False)
```

time: 301 us -> 149 us (0.50)
  the two profiles are of different devices: /device:TPU:0 before, /device:TPU:19 now
where the time goes in v1:
time: 149 us; the launch traced here: 148 us
  Pallas kernels  138 us (93%)
  local copies, waits for them, and re-layouts  9.69 us (7%)
    pallas_call x1, Pallas kernels, body(): pl.pallas_call(functools.partial(kernel, n, slots, blocks, heads), out_sh...  138 us
    reshape x1, local copies, waits for them, and re-layouts, body(): kv = keys_values.reshape(blocks, BLOCK, 2 * feat)  4.42 us
    unnamed x4, local copies, waits for them, and re-layouts  3.89 us

profile of v1, /device:TPU:19, one launch (start us, length us, event | category | flops | bytes accessed | tf_op | source)
XLA Modules:
  0.0 148.5 jit_solution(3812793066503374126)
XLA Ops:
  0.0 0.8 compare_or_fusion.1
  0.8 0.1 copy.10
  0.9 0.6 select_n.43.bias_ref
  1.5 0.8 copy.9
  2.2 0.1 reshape.117
  2.3 0.2 convert_reduce_fusion
  2.5 0.0 copy-start
  2.5 0.1 select_reduce_fusion
  2.6 0.6 broadcast_in_dim.35.tab_ref
  3.2 4.4 %reshape.116.kv_ref = bf16[16,64,1024]{2,1,0:T(8,128)(2,1)} reshape(bf16[1024,2,512]{2,1,0:T(2,128)(2,1)} %param.5) | data formatting | bytes 4194304 | tf_op jit(solution)/shard_map/reshape | solution.py:419
  7.7 0.0 copy-done
  7.7 137.7 %shard_map.46 = bf16[256,4096]{1,0:T(8,128)(2,1)} custom-call(bf16[1024,512]{1,0:T(8,128)(2,1)} %q_ref.1, bf16[16,64,1024]{2,1,0:T(8,128)(2,1)} %reshape.116.kv_ref, s32[8,128]{1,0:T(8,128)} %broadcast_in_dim.35.tab_ref, s32[32]{0:T(128)} %copy-done, f32[32]{0:T(128)} %select_n.43.bias_ref, bf16[512,4096]{1,0:T(8,128)(2,1)} %w_ref.1), custom_call_target="tpu_custom_call" | custom-call | flops 6000000000 | bytes 20000000 | tf_op jit(solution)/shard_map/pallas_call | solution.py:425
  145.4 3.1 %copy.12 = bf16[256,4096]{1,0:T(8,128)(2,1)} copy(bf16[256,4096]{1,0:T(8,128)(2,1)} %shard_map.46) | data formatting | bytes 4194304
  (3 shorter events, 0.0 us)
Async XLA Ops:
  2.5 5.1 %copy-start = (s32[32]{0:T(128)}, s32[32]{0:T(128)S(1)}, u32[]{:S(2)}) copy-start(s32[32]{0:T(128)S(1)} %multiply_add_fusion.slot_ref) | copy-start | bytes 388

commit v2 on v1

--- a/solution.py
+++ b/solution.py
@@ -31,7 +31,10 @@
     tabs,
     tabs_s,
     stage,
-    recv,
+    recv_0,
+    recv_1,
+    recv_2,
+    recv_3,
     m_ref,
     l_ref,
     acc,
@@ -56,9 +59,12 @@
     ws_recv,
     wf_send,
     wf_recv,
+    wy_send,
+    wy_recv,
     att_send,
     att_recv,
 ):
+    recvs = (recv_0, recv_1, recv_2, recv_3)
     me = lax.axis_index("seq")
     h = lax.axis_index("head")
     sib = h + 1 - 2 * lax.rem(h, 2)
@@ -80,10 +86,17 @@
             device_id_type=pl.DeviceIdType.MESH,
         )
 
+    half = n // 2
+    side, place = me // half, lax.rem(me, half)
+    pair = me + 1 - 2 * lax.rem(me, 2)
+
     def peer(i):
-        step = (i + 1) // 2
-        d = n // 2 + step * (2 * lax.rem(i, 2) - 1)
-        return lax.rem(me + d, n)
+        over = 1 - i // half
+        k = lax.rem(i, half) + (1 - over)
+        return lax.rem(side + over, 2) * half + lax.rem(place + k, half)
+
+    def mate(i):
+        return side * half + lax.rem(place + 1 + i, half)
 
     barrier = pltpu.get_barrier_semaphore()
 
@@ -130,23 +143,30 @@
     def final_copy(dest):
         return remote(kv_ref.at[blocks - 1], ends.at[1], final_send.at[dest], ends_recv.at[1], dest, h)
 
+    def first_relay(dest):
+        return remote(ends.at[0], ends.at[0], first_send.at[dest], ends_recv.at[0], dest, h)
+
+    def final_relay(dest):
+        return remote(ends.at[1], ends.at[1], final_send.at[dest], ends_recv.at[1], dest, h)
+
+    def to_mates(copy):
+        def go(i, c):
+            copy(mate(i)).start()
+            return c
+
+        lax.fori_loop(0, half - 1, go, 0)
+
     @pl.when(me == 0)
     def _():
-        def go(i, c):
-            first_copy(peer(i)).start()
-            return c
-
-        lax.fori_loop(0, n - 1, go, 0)
+        first_copy(half).start()
+        to_mates(first_copy)
         ends[0] = kv_ref[0]
         kvp[0] = jnp.zeros_like(kvp[0])
 
     @pl.when(me == n - 1)
     def _():
-        def go(i, c):
-            final_copy(peer(i)).start()
-            return c
-
-        lax.fori_loop(0, n - 1, go, 0)
+        final_copy(half - 1).start()
+        to_mates(final_copy)
         ends[1] = kv_ref[blocks - 1]
         kvp[blocks + 1] = jnp.zeros_like(kvp[0])
 
@@ -158,12 +178,18 @@
     def _():
         to_left().start()
 
+    odd = lax.rem(me, 2)
+
+    def w_span(c):
+        place_c = c + odd * (W_CHUNKS - 1 - 2 * c)
+        return pl.ds(pl.multiple_of(place_c * w_rows, w_rows), w_rows)
+
     def w_piece(g, c):
-        return wall.at[g, pl.ds(c * w_rows, w_rows)]
+        return wall.at[g, w_span(c)]
 
     def wx_copy(g, c):
         return remote(
-            w_ref.at[pl.ds(c * w_rows, w_rows)],
+            w_ref.at[w_span(c)],
             w_piece(g, c),
             wx_send.at[c],
             wx_recv.at[c],
@@ -171,7 +197,7 @@
             across,
         )
 
-    for c in range(W_CHUNKS):
+    for c in range(W_CHUNKS - 1):
         wx_copy(h, c).start()
 
     def tab_wait(i, c):
@@ -184,19 +210,33 @@
     to_smem.start()
     to_smem.wait()
 
-    def rand_copy(s, dest):
-        return remote(stage.at[dest], recv.at[s], rand_send.at[dest], rand_recv.at[s], dest, h)
-
-    def rand_start(i, c):
-        dest = peer(i)
+    def rand_copy(hd, s, dest):
+        return remote(
+            stage.at[hd, dest],
+            recvs[hd].at[s],
+            rand_send.at[hd * n + dest],
+            rand_recv.at[hd * n + s],
+            dest,
+            h,
+        )
+
+    def pick(buf, hd, dest):
         for k in range(slots):
-            stage[dest, k] = kv_ref[tabs_s[dest * 8, me * slots + k]]
-        rand_copy(me, dest).start()
-        return c
-
-    lax.fori_loop(0, n - 1, rand_start, 0)
-    for k in range(slots):
-        recv[me, k] = kv_ref[tabs_s[me * 8, me * slots + k]]
+            block = tabs_s[dest * 8, me * slots + k]
+            buf[k, :, :HEAD_DIM] = kv_ref[block, :, pl.ds(hd * HEAD_DIM, HEAD_DIM)]
+            buf[k, :, HEAD_DIM:] = kv_ref[block, :, pl.ds(feat + hd * HEAD_DIM, HEAD_DIM)]
+
+    for hd in range(heads):
+
+        def rand_start(i, c, hd=hd):
+            dest = peer(i)
+            pick(stage.at[hd, dest], hd, dest)
+            rand_copy(hd, me, dest).start()
+            return c
+
+        lax.fori_loop(0, n - 1, rand_start, 0)
+    for hd in range(heads):
+        pick(recvs[hd].at[me], hd, me)
 
     w_own = pltpu.make_async_copy(w_ref, wall.at[h], w_local)
     w_own.start()
@@ -214,10 +254,18 @@
         to_right().wait_recv()
         first_copy(me).wait_recv()
 
+        @pl.when(me == half)
+        def _():
+            to_mates(first_relay)
+
     @pl.when(me < n - 1)
     def _():
         to_left().wait_recv()
         final_copy(me).wait_recv()
+
+        @pl.when(me == half - 1)
+        def _():
+            to_mates(final_relay)
 
     nt = (((1,), (1,)), ((), ()))
 
@@ -260,37 +308,41 @@
     def wf_copy(g, c):
         return remote(w_piece(g, c), w_piece(g, c), wf_send.at[c], wf_recv.at[c], me, sib)
 
-    def forward(c):
-        wx_copy(across, c).wait_recv()
-        wf_copy(across, c).start()
-
-    for c in range(W_CHUNKS - 1):
-        forward(c)
-
-    def rand_wait(i, c):
-        rand_copy(peer(i), me).wait_recv()
-        return c
-
-    lax.fori_loop(0, n - 1, rand_wait, 0)
+    def wy_copy(span):
+        return remote(wall.at[across, span], wall.at[across, span], wy_send, wy_recv, pair, h)
+
+    last = W_CHUNKS - 1
+
+    def rand_wait(hd):
+        def go(i, c):
+            rand_copy(hd, peer(i), me).wait_recv()
+            return c
+
+        lax.fori_loop(0, n - 1, go, 0)
 
     quarter = blocks // 4
 
-    def far(t):
-        def one(u, c):
-            j = t * quarter + u
-            rows = pl.ds(pl.multiple_of(j * BLOCK, BLOCK), BLOCK)
-            urows = pl.ds(pl.multiple_of(u * BLOCK, BLOCK), BLOCK)
-            s0 = slot_ref[2 * j]
-            s1 = slot_ref[2 * j + 1]
-            col = lax.broadcasted_iota(jnp.int32, (BLOCK, 2 * BLOCK), 1)
-            bias = jnp.where(col < BLOCK, bias_ref[2 * j], bias_ref[2 * j + 1])
-            r0, k0 = s0 // slots, lax.rem(s0, slots)
-            r1, k1 = s1 // slots, lax.rem(s1, slots)
-            for hd in range(heads):
-                kc = pl.ds(hd * HEAD_DIM, HEAD_DIM)
-                vc = pl.ds(feat + hd * HEAD_DIM, HEAD_DIM)
-                keys = jnp.concatenate([recv[r0, k0, :, kc], recv[r1, k1, :, kc]], axis=0)
-                vals = jnp.concatenate([recv[r0, k0, :, vc], recv[r1, k1, :, vc]], axis=0)
+    def att_copy(hd, t, g):
+        return remote(
+            att.at[hd, t], attr.at[hd, g], att_send.at[hd * 4 + t], att_recv.at[hd * 4 + g], me, t
+        )
+
+    def far(hd):
+        kc = pl.ds(hd * HEAD_DIM, HEAD_DIM)
+
+        def one(i, c):
+            t = 2 * lax.rem(h // 2 + 1 + i // 2, 2) + lax.rem(h + i, 2)
+            for u in range(quarter):
+                j = t * quarter + u
+                rows = pl.ds(pl.multiple_of(j * BLOCK, BLOCK), BLOCK)
+                s0 = slot_ref[2 * j]
+                s1 = slot_ref[2 * j + 1]
+                col = lax.broadcasted_iota(jnp.int32, (BLOCK, 2 * BLOCK), 1)
+                bias = jnp.where(col < BLOCK, bias_ref[2 * j], bias_ref[2 * j + 1])
+                r0, k0 = s0 // slots, lax.rem(s0, slots)
+                r1, k1 = s1 // slots, lax.rem(s1, slots)
+                both = jnp.concatenate([recvs[hd][r0, k0], recvs[hd][r1, k1]], axis=0)
+                keys, vals = both[:, :HEAD_DIM], both[:, HEAD_DIM:]
                 s = lax.dot_general(q_ref[rows, kc], keys, nt, preferred_element_type=jnp.float32)
                 s = s * scale + bias
                 m0 = m_ref[rows, kc]
@@ -300,47 +352,72 @@
                 tot = l_ref[rows, kc] * alpha + jnp.sum(p, axis=1, keepdims=True)
                 o = jnp.dot(p.astype(jnp.bfloat16), vals, preferred_element_type=jnp.float32)
                 o = o + acc[rows, kc] * alpha
-                att[t, urows, kc] = (o / tot).astype(jnp.bfloat16)
+                att[hd, t, u * BLOCK : (u + 1) * BLOCK, :] = (o / tot).astype(jnp.bfloat16)
+
+            @pl.when(i != 2)
+            def _():
+                att_copy(hd, t, h).start()
+
             return c
 
-        lax.fori_loop(0, quarter, one, 0)
-
-    def att_copy(t, g):
-        return remote(att.at[t], attr.at[g], att_send.at[t], att_recv.at[g], me, t)
-
-    for t in others:
-        far(t)
-        att_copy(t, h).start()
-    far(h)
-
-    forward(W_CHUNKS - 1)
+        lax.fori_loop(0, 4, one, 0)
+
+    for hd in range(heads):
+        if hd < last:
+            wx_copy(across, hd).wait_recv()
+            wf_copy(across, hd).start()
+        if hd == 0:
+            wy_copy(w_span(0)).start()
+        if hd == last:
+            wy_copy(w_span(last)).wait_recv()
+            wf_copy(across, last).start()
+        rand_wait(hd)
+        far(hd)
+
     w_own.wait()
     ws_copy.wait_recv()
-    att_copy(h, sib).wait_recv()
+    for c in range(W_CHUNKS):
+        wf_copy(across_sib, c).wait_recv()
+    for hd in range(heads):
+        att_copy(hd, h, sib).wait_recv()
+    for hd in range(heads - 1):
+        att_copy(hd, h, across).wait_recv()
+        att_copy(hd, h, across_sib).wait_recv()
 
     tile = 512
     tiles = out_ref.shape[1] // tile
+    early = (heads - 1) * HEAD_DIM
+
+    def joined(buf, g, count):
+        return jnp.concatenate([buf[hd, g] for hd in range(count)], axis=1)
 
     def project_a(i, c):
         cols = pl.ds(pl.multiple_of(i * tile, tile), tile)
-        o = jnp.dot(att[h], wall[h, :, cols], preferred_element_type=jnp.float32)
-        o = o + jnp.dot(attr[sib], wall[sib, :, cols], preferred_element_type=jnp.float32)
+        o = jnp.dot(joined(att, h, heads), wall[h, :, cols], preferred_element_type=jnp.float32)
+        for g, buf, count in (
+            (sib, attr, heads),
+            (across, attr, heads - 1),
+            (across_sib, attr, heads - 1),
+        ):
+            o = o + jnp.dot(
+                joined(buf, g, count),
+                wall[g, : count * HEAD_DIM, cols],
+                preferred_element_type=jnp.float32,
+            )
         oacc[:, cols] = o
         return c
 
     lax.fori_loop(0, tiles, project_a, 0)
-    for c in range(W_CHUNKS):
-        wf_copy(across_sib, c).wait_recv()
-    att_copy(h, across).wait_recv()
-    att_copy(h, across_sib).wait_recv()
+    att_copy(heads - 1, h, across).wait_recv()
+    att_copy(heads - 1, h, across_sib).wait_recv()
 
     def project_b(i, c):
         cols = pl.ds(pl.multiple_of(i * tile, tile), tile)
         o = oacc[:, cols]
-        o = o + jnp.dot(attr[across], wall[across, :, cols], preferred_element_type=jnp.float32)
-        o = o + jnp.dot(
-            attr[across_sib], wall[across_sib, :, cols], preferred_element_type=jnp.float32
-        )
+        for g in (across, across_sib):
+            o = o + jnp.dot(
+                attr[heads - 1, g], wall[g, early:, cols], preferred_element_type=jnp.float32
+            )
         out_ref[:, cols] = o.astype(jnp.bfloat16)
         return c
 
@@ -348,26 +425,36 @@
 
     def drain(i, c):
         tab_copy(me, peer(i)).wait_send()
-        rand_copy(me, peer(i)).wait_send()
+        for hd in range(heads):
+            rand_copy(hd, me, peer(i)).wait_send()
         return c
 
     lax.fori_loop(0, n - 1, drain, 0)
 
+    def from_mates(copy):
+        def go(i, c):
+            copy(mate(i)).wait_send()
+            return c
+
+        lax.fori_loop(0, half - 1, go, 0)
+
     @pl.when(me == 0)
     def _():
-        def go(i, c):
-            first_copy(peer(i)).wait_send()
-            return c
-
-        lax.fori_loop(0, n - 1, go, 0)
+        first_copy(half).wait_send()
+        from_mates(first_copy)
 
     @pl.when(me == n - 1)
     def _():
-        def go(i, c):
-            final_copy(peer(i)).wait_send()
-            return c
-
-        lax.fori_loop(0, n - 1, go, 0)
+        final_copy(half - 1).wait_send()
+        from_mates(final_copy)
+
+    @pl.when(me == half)
+    def _():
+        from_mates(first_relay)
+
+    @pl.when(me == half - 1)
+    def _():
+        from_mates(final_relay)
 
     @pl.when(me < n - 1)
     def _():
@@ -378,11 +465,14 @@
         to_left().wait_send()
 
     for c in range(W_CHUNKS):
-        wx_copy(h, c).wait_send()
+        if c < last:
+            wx_copy(h, c).wait_send()
         wf_copy(across, c).wait_send()
+    wy_copy(w_span(0)).wait_send()
     ws_copy.wait_send()
-    for t in others:
-        att_copy(t, h).wait_send()
+    for hd in range(heads):
+        for t in others:
+            att_copy(hd, t, h).wait_send()
 
 
 def body(queries, keys_values, rand_blocks, w_out):
@@ -432,13 +522,13 @@
             pltpu.VMEM((2, BLOCK, 2 * feat), bf16),
             pltpu.VMEM((n * 8, 128), i32),
             pltpu.SMEM((n * 8, 128), i32),
-            pltpu.VMEM((n, slots, BLOCK, 2 * feat), bf16),
-            pltpu.VMEM((n, slots, BLOCK, 2 * feat), bf16),
+            pltpu.VMEM((heads, n, slots, BLOCK, 2 * HEAD_DIM), bf16),
+            *[pltpu.VMEM((n, slots, BLOCK, 2 * HEAD_DIM), bf16)] * 4,
             pltpu.VMEM((tok_rows, feat), f32),
             pltpu.VMEM((tok_rows, feat), f32),
             pltpu.VMEM((tok_rows, feat), f32),
-            pltpu.VMEM((n_head, rows_out, feat), bf16),
-            pltpu.VMEM((n_head, rows_out, feat), bf16),
+            pltpu.VMEM((heads, n_head, rows_out, HEAD_DIM), bf16),
+            pltpu.VMEM((heads, n_head, rows_out, HEAD_DIM), bf16),
             pltpu.VMEM((n_head, feat, width), bf16),
             pltpu.VMEM((rows_out, width), f32),
             dma((n,)),
@@ -449,8 +539,8 @@
             dma((n,)),
             dma((n,)),
             dma((2,)),
-            dma((n,)),
-            dma((n,)),
+            dma((heads * n,)),
+            dma((heads * n,)),
             dma,
             dma((W_CHUNKS,)),
             dma((W_CHUNKS,)),
@@ -458,8 +548,10 @@
             dma,
             dma((W_CHUNKS,)),
             dma((W_CHUNKS,)),
-            dma((n_head,)),
-            dma((n_head,)),
+            dma,
+            dma,
+            dma((heads * n_head,)),
+            dma((heads * n_head,)),
         ],
         compiler_params=pltpu.CompilerParams(
             collective_id=0, has_side_effects=True, vmem_limit_bytes=60 * 1024 * 1024

time: 149 us -> 144 us (0.966)
  the two profiles are of different devices: /device:TPU:19 before, /device:TPU:0 now
where the time goes in v2:
time: 144 us; the launch traced here: 142 us
  Pallas kernels  132 us (92%)
  local copies, waits for them, and re-layouts  9.69 us (7%)
    pallas_call x1, Pallas kernels, body(): pl.pallas_call(functools.partial(kernel, n, slots, blocks, heads), out_sh...  132 us
    reshape x1, local copies, waits for them, and re-layouts, body(): kv = keys_values.reshape(blocks, BLOCK, 2 * feat)  4.42 us
    unnamed x4, local copies, waits for them, and re-layouts  3.89 us

profile of v2, /device:TPU:0, one launch (start us, length us, event | category | flops | bytes accessed | tf_op | source)
XLA Modules:
  0.0 142.5 jit_solution(9729051671519526959)
XLA Ops:
  0.0 0.8 compare_or_fusion.1
  0.8 0.1 copy.10
  0.9 0.6 select_n.43.bias_ref
  1.5 0.8 copy.9
  2.2 0.1 reshape.117
  2.3 0.2 convert_reduce_fusion
  2.5 0.0 copy-start
  2.5 0.1 select_reduce_fusion
  2.6 0.6 broadcast_in_dim.35.tab_ref
  3.2 4.4 %reshape.116.kv_ref = bf16[16,64,1024]{2,1,0:T(8,128)(2,1)} reshape(bf16[1024,2,512]{2,1,0:T(2,128)(2,1)} %param.5) | data formatting | bytes 4194304 | tf_op jit(solution)/shard_map/reshape | solution.py:509
  7.7 0.0 copy-done
  7.7 131.7 %shard_map.46 = bf16[256,4096]{1,0:T(8,128)(2,1)} custom-call(bf16[1024,512]{1,0:T(8,128)(2,1)} %q_ref.1, bf16[16,64,1024]{2,1,0:T(8,128)(2,1)} %reshape.116.kv_ref, s32[8,128]{1,0:T(8,128)} %broadcast_in_dim.35.tab_ref, s32[32]{0:T(128)} %copy-done, f32[32]{0:T(128)} %select_n.43.bias_ref, bf16[512,4096]{1,0:T(8,128)(2,1)} %w_ref.1), custom_call_target="tpu_custom_call" | custom-call | flops 6000000000 | bytes 20000000 | tf_op jit(solution)/shard_map/pallas_call | solution.py:515
  139.4 3.1 %copy.12 = bf16[256,4096]{1,0:T(8,128)(2,1)} copy(bf16[256,4096]{1,0:T(8,128)(2,1)} %shard_map.46) | data formatting | bytes 4194304
  (3 shorter events, 0.0 us)
Async XLA Ops:
  2.5 5.1 %copy-start = (s32[32]{0:T(128)}, s32[32]{0:T(128)S(1)}, u32[]{:S(2)}) copy-start(s32[32]{0:T(128)S(1)} %multiply_add_fusion.slot_ref) | copy-start | bytes 388

commit v3 on v2

--- a/solution.py
+++ b/solution.py
@@ -90,10 +90,17 @@
     side, place = me // half, lax.rem(me, half)
     pair = me + 1 - 2 * lax.rem(me, 2)
 
+    deep = half // 2
+    level, lane = place // 2, lax.rem(place, 2)
+    inner = lax.rem(level + side + 1, 2)
+
     def peer(i):
-        over = 1 - i // half
-        k = lax.rem(i, half) + (1 - over)
-        return lax.rem(side + over, 2) * half + lax.rem(place + k, half)
+        i = lax.rem(i + inner + n - 2, n - 1)
+        over = 1 - lax.rem(i, 2)
+        k = (i + 1) // 2
+        to_level = lax.rem(level + lax.rem(k, deep), deep)
+        to_lane = lax.rem(lane + k // deep, 2)
+        return lax.rem(side + over, 2) * half + to_level * 2 + to_lane
 
     def mate(i):
         return side * half + lax.rem(place + 1 + i, half)
@@ -362,6 +369,34 @@
 
         lax.fori_loop(0, 4, one, 0)
 
+    tile = 512
+    tiles = out_ref.shape[1] // tile
+    early = (heads - 1) * HEAD_DIM
+
+    def joined(buf, g):
+        return jnp.concatenate([buf[hd, g] for hd in range(heads - 1)], axis=1)
+
+    def project_a(i, c):
+        cols = pl.ds(pl.multiple_of(i * tile, tile), tile)
+        o = jnp.dot(joined(att, h), wall[h, :early, cols], preferred_element_type=jnp.float32)
+        for g in (sib, across, across_sib):
+            o = o + jnp.dot(
+                joined(attr, g), wall[g, :early, cols], preferred_element_type=jnp.float32
+            )
+        oacc[:, cols] = o
+        return c
+
+    def project_b(i, c):
+        cols = pl.ds(pl.multiple_of(i * tile, tile), tile)
+        o = oacc[:, cols]
+        o = o + jnp.dot(att[last, h], wall[h, early:, cols], preferred_element_type=jnp.float32)
+        for g in (sib, across, across_sib):
+            o = o + jnp.dot(
+                attr[last, g], wall[g, early:, cols], preferred_element_type=jnp.float32
+            )
+        out_ref[:, cols] = o.astype(jnp.bfloat16)
+        return c
+
     for hd in range(heads):
         if hd < last:
             wx_copy(across, hd).wait_recv()
@@ -371,56 +406,19 @@
         if hd == last:
             wy_copy(w_span(last)).wait_recv()
             wf_copy(across, last).start()
+            w_own.wait()
+            ws_copy.wait_recv()
+            for c in range(W_CHUNKS):
+                wf_copy(across_sib, c).wait_recv()
+            for e in range(last):
+                for g in others:
+                    att_copy(e, h, g).wait_recv()
+            lax.fori_loop(0, tiles, project_a, 0)
         rand_wait(hd)
         far(hd)
 
-    w_own.wait()
-    ws_copy.wait_recv()
-    for c in range(W_CHUNKS):
-        wf_copy(across_sib, c).wait_recv()
-    for hd in range(heads):
-        att_copy(hd, h, sib).wait_recv()
-    for hd in range(heads - 1):
-        att_copy(hd, h, across).wait_recv()
-        att_copy(hd, h, across_sib).wait_recv()
-
-    tile = 512
-    tiles = out_ref.shape[1] // tile
-    early = (heads - 1) * HEAD_DIM
-
-    def joined(buf, g, count):
-        return jnp.concatenate([buf[hd, g] for hd in range(count)], axis=1)
-
-    def project_a(i, c):
-        cols = pl.ds(pl.multiple_of(i * tile, tile), tile)
-        o = jnp.dot(joined(att, h, heads), wall[h, :, cols], preferred_element_type=jnp.float32)
-        for g, buf, count in (
-            (sib, attr, heads),
-            (across, attr, heads - 1),
-            (across_sib, attr, heads - 1),
-        ):
-            o = o + jnp.dot(
-                joined(buf, g, count),
-                wall[g, : count * HEAD_DIM, cols],
-                preferred_element_type=jnp.float32,
-            )
-        oacc[:, cols] = o
-        return c
-
-    lax.fori_loop(0, tiles, project_a, 0)
-    att_copy(heads - 1, h, across).wait_recv()
-    att_copy(heads - 1, h, across_sib).wait_recv()
-
-    def project_b(i, c):
-        cols = pl.ds(pl.multiple_of(i * tile, tile), tile)
-        o = oacc[:, cols]
-        for g in (across, across_sib):
-            o = o + jnp.dot(
-                attr[heads - 1, g], wall[g, early:, cols], preferred_element_type=jnp.float32
-            )
-        out_ref[:, cols] = o.astype(jnp.bfloat16)
-        return c
-
+    for g in others:
+        att_copy(last, h, g).wait_recv()
     lax.fori_loop(0, tiles, project_b, 0)
 
     def drain(i, c):

time: 144 us -> 146 us (1.014); the launches traced: 142 us -> 146 us
  Pallas kernels: 132 us -> 135 us
    pallas_call x1, Pallas kernels: 132 us -> 135 us  [body(): pl.pallas_call(functools.partial(kernel, n, slots, blocks, heads), out_sh...]
where the time goes in v3:
time: 146 us
  Pallas kernels  135 us (92%)
  local copies, waits for them, and re-layouts  9.69 us (7%)
    pallas_call x1, Pallas kernels, body(): pl.pallas_call(functools.partial(kernel, n, slots, blocks, heads), out_sh...  135 us
    reshape x1, local copies, waits for them, and re-layouts, body(): kv = keys_values.reshape(blocks, BLOCK, 2 * feat)  4.42 us
    unnamed x4, local copies, waits for them, and re-layouts  3.89 us

profile of v3, /device:TPU:0, one launch (start us, length us, event | category | flops | bytes accessed | tf_op | source)
XLA Modules:
  0.0 146.2 jit_solution(4987261839669880998)
XLA Ops:
  0.0 0.8 compare_or_fusion.1
  0.8 0.1 copy.10
  0.9 0.6 select_n.43.bias_ref
  1.5 0.8 copy.9
  2.2 0.1 reshape.117
  2.3 0.2 convert_reduce_fusion
  2.5 0.0 copy-start
  2.5 0.1 select_reduce_fusion
  2.6 0.6 broadcast_in_dim.35.tab_ref
  3.2 4.4 %reshape.116.kv_ref = bf16[16,64,1024]{2,1,0:T(8,128)(2,1)} reshape(bf16[1024,2,512]{2,1,0:T(2,128)(2,1)} %param.5) | data formatting | bytes 4194304 | tf_op jit(solution)/shard_map/reshape | solution.py:507
  7.7 0.0 copy-done
  7.7 135.4 %shard_map.46 = bf16[256,4096]{1,0:T(8,128)(2,1)} custom-call(bf16[1024,512]{1,0:T(8,128)(2,1)} %q_ref.1, bf16[16,64,1024]{2,1,0:T(8,128)(2,1)} %reshape.116.kv_ref, s32[8,128]{1,0:T(8,128)} %broadcast_in_dim.35.tab_ref, s32[32]{0:T(128)} %copy-done, f32[32]{0:T(128)} %select_n.43.bias_ref, bf16[512,4096]{1,0:T(8,128)(2,1)} %w_ref.1), custom_call_target="tpu_custom_call" | custom-call | flops 6000000000 | bytes 20000000 | tf_op jit(solution)/shard_map/pallas_call | solution.py:513
  143.1 3.1 %copy.12 = bf16[256,4096]{1,0:T(8,128)(2,1)} copy(bf16[256,4096]{1,0:T(8,128)(2,1)} %shard_map.46) | data formatting | bytes 4194304
  (3 shorter events, 0.0 us)
Async XLA Ops:
  2.5 5.1 %copy-start = (s32[32]{0:T(128)}, s32[32]{0:T(128)S(1)}, u32[]{:S(2)}) copy-start(s32[32]{0:T(128)S(1)} %multiply_add_fusion.slot_ref) | copy-start | bytes 388

commit v4 on v3

--- a/solution.py
+++ b/solution.py
@@ -92,13 +92,13 @@
 
     deep = half // 2
     level, lane = place // 2, lax.rem(place, 2)
-    inner = lax.rem(level + side + 1, 2)
 
     def peer(i):
-        i = lax.rem(i + inner + n - 2, n - 1)
         over = 1 - lax.rem(i, 2)
         k = (i + 1) // 2
-        to_level = lax.rem(level + lax.rem(k, deep), deep)
+        inward = lax.rem(k, deep)
+        facing = inward + (1 - side) * (deep - 1 - 2 * inward)
+        to_level = over * facing + (1 - over) * lax.rem(level + inward, deep)
         to_lane = lax.rem(lane + k // deep, 2)
         return lax.rem(side + over, 2) * half + to_level * 2 + to_lane
 
@@ -217,6 +217,16 @@
     to_smem.start()
     to_smem.wait()
 
+    @pl.when(me == half)
+    def _():
+        first_copy(me).wait_recv()
+        to_mates(first_relay)
+
+    @pl.when(me == half - 1)
+    def _():
+        final_copy(me).wait_recv()
+        to_mates(final_relay)
+
     def rand_copy(hd, s, dest):
         return remote(
             stage.at[hd, dest],
@@ -259,20 +269,18 @@
     @pl.when(me > 0)
     def _():
         to_right().wait_recv()
-        first_copy(me).wait_recv()
-
-        @pl.when(me == half)
+
+        @pl.when(me != half)
         def _():
-            to_mates(first_relay)
+            first_copy(me).wait_recv()
 
     @pl.when(me < n - 1)
     def _():
         to_left().wait_recv()
-        final_copy(me).wait_recv()
-
-        @pl.when(me == half - 1)
+
+        @pl.when(me != half - 1)
         def _():
-            to_mates(final_relay)
+            final_copy(me).wait_recv()
 
     nt = (((1,), (1,)), ((), ()))
 

time: 146 us -> 129 us (0.88)
  Pallas kernels: 135 us -> 118 us
    pallas_call x1, Pallas kernels: 135 us -> 118 us  [body(): pl.pallas_call(functools.partial(kernel, n, slots, blocks, heads), out_sh...]
where the time goes in v4:
time: 129 us
  Pallas kernels  118 us (91%)
  local copies, waits for them, and re-layouts  9.69 us (8%)
    pallas_call x1, Pallas kernels, body(): pl.pallas_call(functools.partial(kernel, n, slots, blocks, heads), out_sh...  118 us
    reshape x1, local copies, waits for them, and re-layouts, body(): kv = keys_values.reshape(blocks, BLOCK, 2 * feat)  4.42 us
    unnamed x4, local copies, waits for them, and re-layouts  3.89 us

profile of v4, /device:TPU:0, one launch (start us, length us, event | category | flops | bytes accessed | tf_op | source)
XLA Modules:
  0.0 128.8 jit_solution(15860411244006304646)
XLA Ops:
  0.0 0.8 compare_or_fusion.1
  0.8 0.1 copy.10
  0.9 0.6 select_n.43.bias_ref
  1.5 0.8 copy.9
  2.2 0.1 reshape.117
  2.3 0.2 convert_reduce_fusion
  2.5 0.0 copy-start
  2.5 0.1 select_reduce_fusion
  2.6 0.6 broadcast_in_dim.35.tab_ref
  3.2 4.4 %reshape.116.kv_ref = bf16[16,64,1024]{2,1,0:T(8,128)(2,1)} reshape(bf16[1024,2,512]{2,1,0:T(2,128)(2,1)} %param.5) | data formatting | bytes 4194304 | tf_op jit(solution)/shard_map/reshape | solution.py:515
  7.7 0.0 copy-done
  7.7 118.0 %shard_map.46 = bf16[256,4096]{1,0:T(8,128)(2,1)} custom-call(bf16[1024,512]{1,0:T(8,128)(2,1)} %q_ref.1, bf16[16,64,1024]{2,1,0:T(8,128)(2,1)} %reshape.116.kv_ref, s32[8,128]{1,0:T(8,128)} %broadcast_in_dim.35.tab_ref, s32[32]{0:T(128)} %copy-done, f32[32]{0:T(128)} %select_n.43.bias_ref, bf16[512,4096]{1,0:T(8,128)(2,1)} %w_ref.1), custom_call_target="tpu_custom_call" | custom-call | flops 6000000000 | bytes 20000000 | tf_op jit(solution)/shard_map/pallas_call | solution.py:521
  125.7 3.1 %copy.12 = bf16[256,4096]{1,0:T(8,128)(2,1)} copy(bf16[256,4096]{1,0:T(8,128)(2,1)} %shard_map.46) | data formatting | bytes 4194304
  (3 shorter events, 0.0 us)
Async XLA Ops:
  2.5 5.1 %copy-start = (s32[32]{0:T(128)}, s32[32]{0:T(128)S(1)}, u32[]{:S(2)}) copy-start(s32[32]{0:T(128)S(1)} %multiply_add_fusion.slot_ref) | copy-start | bytes 388

commit v5 on v4

--- a/solution.py
+++ b/solution.py
@@ -1,5 +1,4 @@
 import functools
-from functools import reduce
 
 import jax
 import jax.numpy as jnp
@@ -19,13 +18,18 @@
     slots,
     blocks,
     heads,
+    q_hbm,
+    raw_hbm,
+    rb_ref,
+    w_ref,
+    out_ref,
     q_ref,
+    raw_ref,
     kv_ref,
     tab_ref,
-    slot_ref,
-    bias_ref,
-    w_ref,
-    out_ref,
+    out_v,
+    in_sem,
+    out_sem,
     kvp,
     ends,
     tabs,
@@ -105,6 +109,11 @@
     def mate(i):
         return side * half + lax.rem(place + 1 + i, half)
 
+    load_raw = pltpu.make_async_copy(raw_hbm, raw_ref, in_sem.at[0])
+    load_q = pltpu.make_async_copy(q_hbm, q_ref, in_sem.at[1])
+    load_raw.start()
+    load_q.start()
+
     barrier = pltpu.get_barrier_semaphore()
 
     def greet(i, c):
@@ -116,6 +125,24 @@
     lax.fori_loop(0, n - 1, greet, 0)
     for g in others:
         pl.semaphore_signal(barrier, inc=1, device_id=(me, g), device_id_type=pl.DeviceIdType.MESH)
+    entries = 2 * blocks
+    lanes = lax.broadcasted_iota(jnp.int32, (entries, 128), 1)
+    subs = lax.broadcasted_iota(jnp.int32, (entries, 128), 0)
+    owner_row = jnp.full((entries, 128), -1, jnp.int32)
+    owner_col = jnp.zeros((entries, 128), jnp.int32)
+    offset_col = jnp.zeros((entries, 128), jnp.int32)
+    for e in range(entries):
+        named = rb_ref[e % 2, e // 2]
+        owner = named // blocks
+        owner_row = jnp.where(lanes == e, owner, owner_row)
+        owner_col = jnp.where(subs == e, owner, owner_col)
+        offset_col = jnp.where(subs == e, named - owner * blocks, offset_col)
+    ahead = jnp.where((owner_row == owner_col) & (lanes < subs), 1, 0)
+    slot_col = owner_col * slots + jnp.sum(ahead, axis=1, keepdims=True)
+    outgoing = jnp.sum(jnp.where(slot_col == lanes, offset_col, 0), axis=0, keepdims=True)
+    tab_ref[...] = jnp.broadcast_to(outgoing, (8, 128))
+    tabs[n * 8 : n * 8 + entries, :] = slot_col
+
     pl.semaphore_wait(barrier, n - 1 + 3)
 
     def tab_copy(s, dest):
@@ -128,6 +155,15 @@
         return c
 
     lax.fori_loop(0, n - 1, tab_start, 0)
+
+    load_raw.wait()
+
+    def unpack(j):
+        kv_ref[j, :, :feat] = raw_ref[j, :, 0, :]
+        kv_ref[j, :, feat:] = raw_ref[j, :, 1, :]
+
+    unpack(0)
+    unpack(blocks - 1)
 
     def to_right():
         return remote(
@@ -185,6 +221,12 @@
     def _():
         to_left().start()
 
+    def unpack_one(j, c):
+        unpack(j)
+        return c
+
+    lax.fori_loop(1, blocks - 1, unpack_one, 0)
+
     odd = lax.rem(me, 2)
 
     def w_span(c):
@@ -265,6 +307,7 @@
         return c
 
     lax.fori_loop(0, blocks, fill, 0)
+    load_q.wait()
 
     @pl.when(me > 0)
     def _():
@@ -350,10 +393,19 @@
             for u in range(quarter):
                 j = t * quarter + u
                 rows = pl.ds(pl.multiple_of(j * BLOCK, BLOCK), BLOCK)
-                s0 = slot_ref[2 * j]
-                s1 = slot_ref[2 * j + 1]
+                s0 = tabs_s[n * 8 + 2 * j, 0]
+                s1 = tabs_s[n * 8 + 2 * j + 1, 0]
+                block = me * blocks + j
+                n0, n1 = rb_ref[0, j], rb_ref[1, j]
+
+                def clash(x, block=block):
+                    near_by = (x >= block - 1) & (x <= block + 1)
+                    return near_by | (x == 0) | (x == total_blocks - 1)
+
+                b0 = jnp.where(clash(n0), NEG, 0.0)
+                b1 = jnp.where(clash(n1) | (n1 == n0), NEG, 0.0)
                 col = lax.broadcasted_iota(jnp.int32, (BLOCK, 2 * BLOCK), 1)
-                bias = jnp.where(col < BLOCK, bias_ref[2 * j], bias_ref[2 * j + 1])
+                bias = jnp.where(col < BLOCK, b0, b1)
                 r0, k0 = s0 // slots, lax.rem(s0, slots)
                 r1, k1 = s1 // slots, lax.rem(s1, slots)
                 both = jnp.concatenate([recvs[hd][r0, k0], recvs[hd][r1, k1]], axis=0)
@@ -394,15 +446,29 @@
         oacc[:, cols] = o
         return c
 
+    def tail(bufs, cols):
+        rows = jnp.concatenate([buf[last, g] for buf, g in bufs], axis=1)
+        weights = jnp.concatenate([wall[g, early:, cols] for buf, g in bufs], axis=0)
+        return oacc[:, cols] + jnp.dot(rows, weights, preferred_element_type=jnp.float32)
+
     def project_b(i, c):
         cols = pl.ds(pl.multiple_of(i * tile, tile), tile)
-        o = oacc[:, cols]
-        o = o + jnp.dot(att[last, h], wall[h, early:, cols], preferred_element_type=jnp.float32)
-        for g in (sib, across, across_sib):
-            o = o + jnp.dot(
-                attr[last, g], wall[g, early:, cols], preferred_element_type=jnp.float32
-            )
-        out_ref[:, cols] = o.astype(jnp.bfloat16)
+        oacc[:, cols] = tail(((att, h), (attr, sib)), cols)
+        return c
+
+    def out_copy(i):
+        cols = pl.ds(pl.multiple_of(i * tile, tile), tile)
+        return pltpu.make_async_copy(out_v.at[:, cols], out_ref.at[:, cols], out_sem.at[i])
+
+    def project_c(i, c):
+        cols = pl.ds(pl.multiple_of(i * tile, tile), tile)
+        o = tail(((attr, across), (attr, across_sib)), cols)
+        out_v[:, cols] = o.astype(jnp.bfloat16)
+        out_copy(i).start()
+        return c
+
+    def out_wait(i, c):
+        out_copy(i).wait()
         return c
 
     for hd in range(heads):
@@ -425,9 +491,11 @@
         rand_wait(hd)
         far(hd)
 
-    for g in others:
-        att_copy(last, h, g).wait_recv()
+    att_copy(last, h, sib).wait_recv()
     lax.fori_loop(0, tiles, project_b, 0)
+    att_copy(last, h, across).wait_recv()
+    att_copy(last, h, across_sib).wait_recv()
+    lax.fori_loop(0, tiles, project_c, 0)
 
     def drain(i, c):
         tab_copy(me, peer(i)).wait_send()
@@ -479,6 +547,7 @@
     for hd in range(heads):
         for t in others:
             att_copy(hd, t, h).wait_send()
+    lax.fori_loop(0, tiles, out_wait, 0)
 
 
 def body(queries, keys_values, rand_blocks, w_out):
@@ -487,47 +556,31 @@
     blocks = tok_rows // BLOCK
     n = lax.axis_size("seq")
     n_head = lax.axis_size("head")
-    all_blocks = blocks * n
-    position = lax.axis_index("seq")
     entries = rand_blocks.shape[0] * rand_blocks.shape[1]
     slots = max(1, entries // n)
     width = w_out.shape[1]
-
-    flat = rand_blocks.reshape(entries)
-    owner = flat // blocks
-    offset = flat % blocks
-    earlier = jnp.arange(entries)[:, None] > jnp.arange(entries)[None, :]
-    rank = jnp.sum((owner[:, None] == owner[None, :]) & earlier, axis=1)
-    slot = (owner * slots + rank).astype(jnp.int32)
-    placed = slot[:, None] == jnp.arange(128)[None, :]
-    outgoing = jnp.sum(jnp.where(placed, offset[:, None], 0), axis=0).astype(jnp.int32)
-    table = jnp.broadcast_to(outgoing[None, :], (8, 128))
-
-    ids = position * blocks + jnp.arange(blocks, dtype=jnp.int32)
-    taken = [ids - 1, ids, ids + 1, jnp.zeros_like(ids), jnp.zeros_like(ids) + (all_blocks - 1)]
-    flags = []
-    for column in range(rand_blocks.shape[1]):
-        chosen = rand_blocks[:, column]
-        flags.append(reduce(jnp.logical_or, [chosen == other for other in taken]))
-        taken.append(chosen)
-    bias = jnp.where(jnp.stack(flags, axis=1), NEG, 0.0).astype(jnp.float32).reshape(entries)
-
-    kv = keys_values.reshape(blocks, BLOCK, 2 * feat)
-    vmem = pl.BlockSpec(memory_space=pltpu.VMEM)
-    smem = pl.BlockSpec(memory_space=pltpu.SMEM)
+    kv = keys_values.reshape(blocks, BLOCK, 2, feat)
+    anywhere = pl.BlockSpec(memory_space=pl.ANY)
     bf16, f32, i32 = jnp.bfloat16, jnp.float32, jnp.int32
     rows_out = tok_rows // n_head
     dma = pltpu.SemaphoreType.DMA
     return pl.pallas_call(
         functools.partial(kernel, n, slots, blocks, heads),
         out_shape=jax.ShapeDtypeStruct((rows_out, width), bf16),
-        in_specs=[vmem, vmem, vmem, smem, smem, pl.BlockSpec(memory_space=pl.ANY)],
-        out_specs=vmem,
+        in_specs=[anywhere, anywhere, pl.BlockSpec(memory_space=pltpu.SMEM), anywhere],
+        out_specs=anywhere,
         scratch_shapes=[
+            pltpu.VMEM((tok_rows, feat), bf16),
+            pltpu.VMEM((blocks, BLOCK, 2, feat), bf16),
+            pltpu.VMEM((blocks, BLOCK, 2 * feat), bf16),
+            pltpu.VMEM((8, 128), i32),
+            pltpu.VMEM((rows_out, width), bf16),
+            dma((2,)),
+            dma((width // 512,)),
             pltpu.VMEM((blocks + 2, BLOCK, 2 * feat), bf16),
             pltpu.VMEM((2, BLOCK, 2 * feat), bf16),
-            pltpu.VMEM((n * 8, 128), i32),
-            pltpu.SMEM((n * 8, 128), i32),
+            pltpu.VMEM((n * 8 + entries, 128), i32),
+            pltpu.SMEM((n * 8 + entries, 128), i32),
             pltpu.VMEM((heads, n, slots, BLOCK, 2 * HEAD_DIM), bf16),
             *[pltpu.VMEM((n, slots, BLOCK, 2 * HEAD_DIM), bf16)] * 4,
             pltpu.VMEM((tok_rows, feat), f32),
@@ -565,7 +618,7 @@
         cost_estimate=pl.CostEstimate(
             flops=6_000_000_000, bytes_accessed=20_000_000, transcendentals=2_000_000
         ),
-    )(queries, kv, table, slot, bias, w_out)
+    )(queries, kv, rand_blocks.T, w_out)
 
 
 def solution(mesh):

time: 129 us -> 120 us (0.930)
  local copies, waits for them, and re-layouts: 9.69 us -> 3.13 us
  Pallas kernels: 118 us -> 116 us
    reshape x2 -> x0, local copies, waits for them, and re-layouts: 4.51 us -> none  [the longest x1 4.42 us: body(): kv = keys_values.reshape(blocks, BLOCK, 2 * feat)]
    pallas_call x1, Pallas kernels: 118 us -> 116 us  [body(): pl.pallas_call(functools.partial(kernel, n, slots, blocks, heads), out_sh...]
    unnamed x4 -> x1, local copies, waits for them, and re-layouts: 3.89 us -> 3.13 us
where the time goes in v5:
time: 120 us; the launch traced here: 119 us
  Pallas kernels  116 us (97%)
  local copies, waits for them, and re-layouts  3.13 us (3%)
    pallas_call x1, Pallas kernels, body(): pl.pallas_call(functools.partial(kernel, n, slots, blocks, heads), out_sh...  116 us
    unnamed x1, local copies, waits for them, and re-layouts  3.13 us

profile of v5, /device:TPU:0, one launch (start us, length us, event | category | flops | bytes accessed | tf_op | source)
XLA Modules:
  0.0 119.0 jit_solution(7849699496040859812)
XLA Ops:
  0.0 115.9 %shard_map.46 = bf16[256,4096]{1,0:T(8,128)(2,1)} custom-call(bf16[1024,512]{1,0:T(8,128)(2,1)} %q_hbm.1, bf16[16,64,2,512]{3,2,1,0:T(2,128)(2,1)} %bitcast.2, s32[2,16]{1,0:T(2,128)} %bitcast.3, bf16[512,4096]{1,0:T(8,128)(2,1)} %w_ref.1), custom_call_target="tpu_custom_call" | custom-call | flops 6000000000 | bytes 20000000 | tf_op jit(solution)/shard_map/pallas_call | solution.py:567
  115.9 3.1 %copy.6 = bf16[256,4096]{1,0:T(8,128)(2,1)} copy(bf16[256,4096]{1,0:T(8,128)(2,1)} %shard_map.46) | data formatting | bytes 4194304

commit v6 on v5

--- a/solution.py
+++ b/solution.py
@@ -39,6 +39,10 @@
     recv_1,
     recv_2,
     recv_3,
+    recv_4,
+    stage_3,
+    stage_4,
+    p_ref,
     m_ref,
     l_ref,
     acc,
@@ -68,7 +72,10 @@
     att_send,
     att_recv,
 ):
-    recvs = (recv_0, recv_1, recv_2, recv_3)
+    recvs = (recv_0, recv_1, recv_2, recv_3, recv_4)
+    stages = (stage.at[0], stage.at[1], stage.at[2], stage_3, stage_4)
+    parts = heads + 1
+    last = heads - 1
     me = lax.axis_index("seq")
     h = lax.axis_index("head")
     sib = h + 1 - 2 * lax.rem(h, 2)
@@ -271,7 +278,7 @@
 
     def rand_copy(hd, s, dest):
         return remote(
-            stage.at[hd, dest],
+            stages[hd].at[dest],
             recvs[hd].at[s],
             rand_send.at[hd * n + dest],
             rand_recv.at[hd * n + s],
@@ -279,22 +286,28 @@
             h,
         )
 
-    def pick(buf, hd, dest):
+    def pick(buf, part, dest):
+        hd = min(part, last)
         for k in range(slots):
             block = tabs_s[dest * 8, me * slots + k]
-            buf[k, :, :HEAD_DIM] = kv_ref[block, :, pl.ds(hd * HEAD_DIM, HEAD_DIM)]
-            buf[k, :, HEAD_DIM:] = kv_ref[block, :, pl.ds(feat + hd * HEAD_DIM, HEAD_DIM)]
-
-    for hd in range(heads):
+            keys = kv_ref[block, :, pl.ds(hd * HEAD_DIM, HEAD_DIM)]
+            vals = kv_ref[block, :, pl.ds(feat + hd * HEAD_DIM, HEAD_DIM)]
+            if part < last:
+                buf[k, :, :HEAD_DIM] = keys
+                buf[k, :, HEAD_DIM:] = vals
+            else:
+                buf[k] = keys if part == last else vals
+
+    for hd in range(parts):
 
         def rand_start(i, c, hd=hd):
             dest = peer(i)
-            pick(stage.at[hd, dest], hd, dest)
+            pick(stages[hd].at[dest], hd, dest)
             rand_copy(hd, me, dest).start()
             return c
 
         lax.fori_loop(0, n - 1, rand_start, 0)
-    for hd in range(heads):
+    for hd in range(parts):
         pick(recvs[hd].at[me], hd, me)
 
     w_own = pltpu.make_async_copy(w_ref, wall.at[h], w_local)
@@ -369,8 +382,6 @@
     def wy_copy(span):
         return remote(wall.at[across, span], wall.at[across, span], wy_send, wy_recv, pair, h)
 
-    last = W_CHUNKS - 1
-
     def rand_wait(hd):
         def go(i, c):
             rand_copy(hd, peer(i), me).wait_recv()
@@ -385,49 +396,87 @@
             att.at[hd, t], attr.at[hd, g], att_send.at[hd * 4 + t], att_recv.at[hd * 4 + g], me, t
         )
 
+    def places(j):
+        s0 = tabs_s[n * 8 + 2 * j, 0]
+        s1 = tabs_s[n * 8 + 2 * j + 1, 0]
+        return (s0 // slots, lax.rem(s0, slots)), (s1 // slots, lax.rem(s1, slots))
+
+    def gathered(part, j):
+        (r0, k0), (r1, k1) = places(j)
+        return jnp.concatenate([recvs[part][r0, k0], recvs[part][r1, k1]], axis=0)
+
+    def weigh(hd, j, keys):
+        kc = pl.ds(hd * HEAD_DIM, HEAD_DIM)
+        rows = pl.ds(pl.multiple_of(j * BLOCK, BLOCK), BLOCK)
+        block = me * blocks + j
+        n0, n1 = rb_ref[0, j], rb_ref[1, j]
+
+        def clash(x):
+            near_by = (x >= block - 1) & (x <= block + 1)
+            return near_by | (x == 0) | (x == total_blocks - 1)
+
+        b0 = jnp.where(clash(n0), NEG, 0.0)
+        b1 = jnp.where(clash(n1) | (n1 == n0), NEG, 0.0)
+        col = lax.broadcasted_iota(jnp.int32, (BLOCK, 2 * BLOCK), 1)
+        bias = jnp.where(col < BLOCK, b0, b1)
+        s = lax.dot_general(q_ref[rows, kc], keys, nt, preferred_element_type=jnp.float32)
+        s = s * scale + bias
+        m0 = m_ref[rows, kc]
+        m = jnp.maximum(m0, jnp.max(s, axis=1, keepdims=True))
+        alpha = jnp.exp(m0 - m)
+        p = jnp.exp(s - m)
+        tot = l_ref[rows, kc] * alpha + jnp.sum(p, axis=1, keepdims=True)
+        return p.astype(jnp.bfloat16), acc[rows, kc] * alpha, tot
+
+    def finish(hd, t, u, p, vals, base, tot):
+        o = jnp.dot(p, vals, preferred_element_type=jnp.float32) + base
+        att[hd, t, u * BLOCK : (u + 1) * BLOCK, :] = (o / tot).astype(jnp.bfloat16)
+
+    def each_pair(hd, do):
+        def one(i, c):
+            ts = [2 * lax.rem(h // 2 + 1 + i, 2) + lax.rem(h + v, 2) for v in range(2)]
+            for t in ts:
+                for u in range(quarter):
+                    do(t, u, t * quarter + u)
+            if hd is not None:
+
+                @pl.when(i == 0)
+                def _():
+                    att_copy(hd, ts[0], h).start()
+
+                att_copy(hd, ts[1], h).start()
+            return c
+
+        lax.fori_loop(0, 2, one, 0)
+
     def far(hd):
-        kc = pl.ds(hd * HEAD_DIM, HEAD_DIM)
-
-        def one(i, c):
-            t = 2 * lax.rem(h // 2 + 1 + i // 2, 2) + lax.rem(h + i, 2)
-            for u in range(quarter):
-                j = t * quarter + u
-                rows = pl.ds(pl.multiple_of(j * BLOCK, BLOCK), BLOCK)
-                s0 = tabs_s[n * 8 + 2 * j, 0]
-                s1 = tabs_s[n * 8 + 2 * j + 1, 0]
-                block = me * blocks + j
-                n0, n1 = rb_ref[0, j], rb_ref[1, j]
-
-                def clash(x, block=block):
-                    near_by = (x >= block - 1) & (x <= block + 1)
-                    return near_by | (x == 0) | (x == total_blocks - 1)
-
-                b0 = jnp.where(clash(n0), NEG, 0.0)
-                b1 = jnp.where(clash(n1) | (n1 == n0), NEG, 0.0)
-                col = lax.broadcasted_iota(jnp.int32, (BLOCK, 2 * BLOCK), 1)
-                bias = jnp.where(col < BLOCK, b0, b1)
-                r0, k0 = s0 // slots, lax.rem(s0, slots)
-                r1, k1 = s1 // slots, lax.rem(s1, slots)
-                both = jnp.concatenate([recvs[hd][r0, k0], recvs[hd][r1, k1]], axis=0)
-                keys, vals = both[:, :HEAD_DIM], both[:, HEAD_DIM:]
-                s = lax.dot_general(q_ref[rows, kc], keys, nt, preferred_element_type=jnp.float32)
-                s = s * scale + bias
-                m0 = m_ref[rows, kc]
-                m = jnp.maximum(m0, jnp.max(s, axis=1, keepdims=True))
-                alpha = jnp.exp(m0 - m)
-                p = jnp.exp(s - m)
-                tot = l_ref[rows, kc] * alpha + jnp.sum(p, axis=1, keepdims=True)
-                o = jnp.dot(p.astype(jnp.bfloat16), vals, preferred_element_type=jnp.float32)
-                o = o + acc[rows, kc] * alpha
-                att[hd, t, u * BLOCK : (u + 1) * BLOCK, :] = (o / tot).astype(jnp.bfloat16)
-
-            @pl.when(i != 2)
-            def _():
-                att_copy(hd, t, h).start()
-
-            return c
-
-        lax.fori_loop(0, 4, one, 0)
+        def do(t, u, j):
+            both = gathered(hd, j)
+            p, base, tot = weigh(hd, j, both[:, :HEAD_DIM])
+            finish(hd, t, u, p, both[:, HEAD_DIM:], base, tot)
+
+        each_pair(hd, do)
+
+    def last_keys():
+        kc = pl.ds(last * HEAD_DIM, HEAD_DIM)
+
+        def do(t, u, j):
+            rows = pl.ds(pl.multiple_of(j * BLOCK, BLOCK), BLOCK)
+            p, base, tot = weigh(last, j, gathered(last, j))
+            p_ref[rows, :] = p
+            acc[rows, kc] = base
+            l_ref[rows, kc] = tot
+
+        each_pair(None, do)
+
+    def last_values():
+        kc = pl.ds(last * HEAD_DIM, HEAD_DIM)
+
+        def do(t, u, j):
+            rows = pl.ds(pl.multiple_of(j * BLOCK, BLOCK), BLOCK)
+            finish(last, t, u, p_ref[rows, :], gathered(heads, j), acc[rows, kc], l_ref[rows, kc])
+
+        each_pair(last, do)
 
     tile = 512
     tiles = out_ref.shape[1] // tile
@@ -489,7 +538,11 @@
                     att_copy(e, h, g).wait_recv()
             lax.fori_loop(0, tiles, project_a, 0)
         rand_wait(hd)
-        far(hd)
+        if hd < last:
+            far(hd)
+    last_keys()
+    rand_wait(heads)
+    last_values()
 
     att_copy(last, h, sib).wait_recv()
     lax.fori_loop(0, tiles, project_b, 0)
@@ -499,7 +552,7 @@
 
     def drain(i, c):
         tab_copy(me, peer(i)).wait_send()
-        for hd in range(heads):
+        for hd in range(parts):
             rand_copy(hd, me, peer(i)).wait_send()
         return c
 
@@ -548,6 +601,20 @@
         for t in others:
             att_copy(hd, t, h).wait_send()
     lax.fori_loop(0, tiles, out_wait, 0)
+
+
+def hand_over(src, dst, sem):
+    rows = src.shape[0] // 8
+    copies = [
+        pltpu.make_async_copy(
+            src.at[pl.ds(i * rows, rows)], dst.at[pl.ds(i * rows, rows)], sem.at[i]
+        )
+        for i in range(8)
+    ]
+    for copy in copies:
+        copy.start()
+    for copy in copies:
+        copy.wait()
 
 
 def body(queries, keys_values, rand_blocks, w_out):
@@ -564,7 +631,7 @@
     bf16, f32, i32 = jnp.bfloat16, jnp.float32, jnp.int32
     rows_out = tok_rows // n_head
     dma = pltpu.SemaphoreType.DMA
-    return pl.pallas_call(
+    mixed = pl.pallas_call(
         functools.partial(kernel, n, slots, blocks, heads),
         out_shape=jax.ShapeDtypeStruct((rows_out, width), bf16),
         in_specs=[anywhere, anywhere, pl.BlockSpec(memory_space=pltpu.SMEM), anywhere],
@@ -581,8 +648,10 @@
             pltpu.VMEM((2, BLOCK, 2 * feat), bf16),
             pltpu.VMEM((n * 8 + entries, 128), i32),
             pltpu.SMEM((n * 8 + entries, 128), i32),
-            pltpu.VMEM((heads, n, slots, BLOCK, 2 * HEAD_DIM), bf16),
-            *[pltpu.VMEM((n, slots, BLOCK, 2 * HEAD_DIM), bf16)] * 4,
+            pltpu.VMEM((heads - 1, n, slots, BLOCK, 2 * HEAD_DIM), bf16),
+            *[pltpu.VMEM((n, slots, BLOCK, 2 * HEAD_DIM), bf16)] * 3,
+            *[pltpu.VMEM((n, slots, BLOCK, HEAD_DIM), bf16)] * 4,
+            pltpu.VMEM((tok_rows, HEAD_DIM), bf16),
             pltpu.VMEM((tok_rows, feat), f32),
             pltpu.VMEM((tok_rows, feat), f32),
             pltpu.VMEM((tok_rows, feat), f32),
@@ -598,8 +667,8 @@
             dma((n,)),
             dma((n,)),
             dma((2,)),
-            dma((heads * n,)),
-            dma((heads * n,)),
+            dma(((heads + 1) * n,)),
+            dma(((heads + 1) * n,)),
             dma,
             dma((W_CHUNKS,)),
             dma((W_CHUNKS,)),
@@ -619,6 +688,13 @@
             flops=6_000_000_000, bytes_accessed=20_000_000, transcendentals=2_000_000
         ),
     )(queries, kv, rand_blocks.T, w_out)
+    return pl.pallas_call(
+        hand_over,
+        out_shape=jax.ShapeDtypeStruct((rows_out, width), bf16),
+        in_specs=[anywhere],
+        out_specs=anywhere,
+        scratch_shapes=[dma((8,))],
+    )(mixed)
 
 
 def solution(mesh):

time: 120 us -> 179 us (1.49)
  Pallas kernels: 116 us -> 179 us
  local copies, waits for them, and re-layouts: 3.13 us -> 0 us
    pallas_call x0 -> x1, Pallas kernels: none -> 64.7 us  [body(): pl.pallas_call(hand_over, out_shape=jax.ShapeDtypeStruct((rows_out, width...]
    unnamed x1 -> x0, local copies, waits for them, and re-layouts: 3.13 us -> none
    pallas_call x1, Pallas kernels: 116 us -> 114 us  [body(): pl.pallas_call(functools.partial(kernel, n, slots, blocks, heads), out_sh...]
where the time goes in v6:
time: 179 us
  Pallas kernels  179 us (100%)
    pallas_call x1, Pallas kernels, body(): pl.pallas_call(functools.partial(kernel, n, slots, blocks, heads), out_sh...  114 us
    pallas_call x1, Pallas kernels, body(): pl.pallas_call(hand_over, out_shape=jax.ShapeDtypeStruct((rows_out, width...  64.7 us

profile of v6, /device:TPU:0, one launch (start us, length us, event | category | flops | bytes accessed | tf_op | source)
XLA Modules:
  0.0 178.8 jit_solution(7127302733421078701)
XLA Ops:
  0.0 114.0 %shard_map.46.src = bf16[256,4096]{1,0:T(8,128)(2,1)} custom-call(bf16[1024,512]{1,0:T(8,128)(2,1)} %q_hbm.1, bf16[16,64,2,512]{3,2,1,0:T(2,128)(2,1)} %bitcast.2, s32[2,16]{1,0:T(2,128)} %bitcast.3, bf16[512,4096]{1,0:T(8,128)(2,1)} %w_ref.1), custom_call_target="tpu_custom_call" | custom-call | flops 6000000000 | bytes 20000000 | tf_op jit(solution)/shard_map/pallas_call | solution.py:634
  114.1 64.7 %shard_map.47 = bf16[256,4096]{1,0:T(8,128)(2,1)} custom-call(bf16[256,4096]{1,0:T(8,128)(2,1)} %shard_map.46.src), custom_call_target="tpu_custom_call" | custom-call | tf_op jit(solution)/shard_map/pallas_call | solution.py:691

commit v7 on v6

--- a/solution.py
+++ b/solution.py
@@ -228,12 +228,6 @@
     def _():
         to_left().start()
 
-    def unpack_one(j, c):
-        unpack(j)
-        return c
-
-    lax.fori_loop(1, blocks - 1, unpack_one, 0)
-
     odd = lax.rem(me, 2)
 
     def w_span(c):
@@ -290,8 +284,12 @@
         hd = min(part, last)
         for k in range(slots):
             block = tabs_s[dest * 8, me * slots + k]
-            keys = kv_ref[block, :, pl.ds(hd * HEAD_DIM, HEAD_DIM)]
-            vals = kv_ref[block, :, pl.ds(feat + hd * HEAD_DIM, HEAD_DIM)]
+            if part == 0:
+                keys = raw_ref[block, :, 0, pl.ds(hd * HEAD_DIM, HEAD_DIM)]
+                vals = raw_ref[block, :, 1, pl.ds(hd * HEAD_DIM, HEAD_DIM)]
+            else:
+                keys = kv_ref[block, :, pl.ds(hd * HEAD_DIM, HEAD_DIM)]
+                vals = kv_ref[block, :, pl.ds(feat + hd * HEAD_DIM, HEAD_DIM)]
             if part < last:
                 buf[k, :, :HEAD_DIM] = keys
                 buf[k, :, HEAD_DIM:] = vals
@@ -307,6 +305,13 @@
             return c
 
         lax.fori_loop(0, n - 1, rand_start, 0)
+        if hd == 0:
+
+            def unpack_one(j, c):
+                unpack(j)
+                return c
+
+            lax.fori_loop(1, blocks - 1, unpack_one, 0)
     for hd in range(parts):
         pick(recvs[hd].at[me], hd, me)
 
@@ -603,18 +608,24 @@
     lax.fori_loop(0, tiles, out_wait, 0)
 
 
-def hand_over(src, dst, sem):
+def hand_over(src, dst, held, in_sem, out_sem):
     rows = src.shape[0] // 8
-    copies = [
-        pltpu.make_async_copy(
-            src.at[pl.ds(i * rows, rows)], dst.at[pl.ds(i * rows, rows)], sem.at[i]
-        )
-        for i in range(8)
-    ]
-    for copy in copies:
-        copy.start()
-    for copy in copies:
-        copy.wait()
+
+    def arrive(i):
+        span = pl.ds(i * rows, rows)
+        return pltpu.make_async_copy(src.at[span], held.at[span], in_sem.at[i])
+
+    def leave(i):
+        span = pl.ds(i * rows, rows)
+        return pltpu.make_async_copy(held.at[span], dst.at[span], out_sem.at[i])
+
+    for i in range(8):
+        arrive(i).start()
+    for i in range(8):
+        arrive(i).wait()
+        leave(i).start()
+    for i in range(8):
+        leave(i).wait()
 
 
 def body(queries, keys_values, rand_blocks, w_out):
@@ -693,7 +704,7 @@
         out_shape=jax.ShapeDtypeStruct((rows_out, width), bf16),
         in_specs=[anywhere],
         out_specs=anywhere,
-        scratch_shapes=[dma((8,))],
+        scratch_shapes=[pltpu.VMEM((rows_out, width), bf16), dma((8,)), dma((8,))],
     )(mixed)
 
 

time: 179 us -> 118 us (0.66)
  Pallas kernels: 179 us -> 117 us
    pallas_call x1, Pallas kernels: 64.7 us -> 2.39 us  [body(): pl.pallas_call(hand_over, out_shape=jax.ShapeDtypeStruct((rows_out, width...]
where the time goes in v7:
time: 118 us; the launch traced here: 117 us
  Pallas kernels  117 us (99%)
    pallas_call x1, Pallas kernels, body(): pl.pallas_call(functools.partial(kernel, n, slots, blocks, heads), out_sh...  115 us
    pallas_call x1, Pallas kernels, body(): pl.pallas_call(hand_over, out_shape=jax.ShapeDtypeStruct((rows_out, width...  2.39 us

profile of v7, /device:TPU:0, one launch (start us, length us, event | category | flops | bytes accessed | tf_op | source)
XLA Modules:
  0.0 117.2 jit_solution(16536309185805513578)
XLA Ops:
  0.0 114.8 %shard_map.46.src = bf16[256,4096]{1,0:T(8,128)(2,1)} custom-call(bf16[1024,512]{1,0:T(8,128)(2,1)} %q_hbm.1, bf16[16,64,2,512]{3,2,1,0:T(2,128)(2,1)} %bitcast.2, s32[2,16]{1,0:T(2,128)} %bitcast.3, bf16[512,4096]{1,0:T(8,128)(2,1)} %w_ref.1), custom_call_target="tpu_custom_call" | custom-call | flops 6000000000 | bytes 20000000 | tf_op jit(solution)/shard_map/pallas_call | solution.py:645
  114.8 2.4 %shard_map.47 = bf16[256,4096]{1,0:T(8,128)(2,1)} custom-call(bf16[256,4096]{1,0:T(8,128)(2,1)} %shard_map.46.src), custom_call_target="tpu_custom_call" | custom-call | tf_op jit(solution)/shard_map/pallas_call | solution.py:702

commit v8 on v7

--- a/solution.py
+++ b/solution.py
@@ -27,9 +27,7 @@
     raw_ref,
     kv_ref,
     tab_ref,
-    out_v,
     in_sem,
-    out_sem,
     kvp,
     ends,
     tabs,
@@ -510,19 +508,10 @@
         oacc[:, cols] = tail(((att, h), (attr, sib)), cols)
         return c
 
-    def out_copy(i):
-        cols = pl.ds(pl.multiple_of(i * tile, tile), tile)
-        return pltpu.make_async_copy(out_v.at[:, cols], out_ref.at[:, cols], out_sem.at[i])
-
     def project_c(i, c):
         cols = pl.ds(pl.multiple_of(i * tile, tile), tile)
         o = tail(((attr, across), (attr, across_sib)), cols)
-        out_v[:, cols] = o.astype(jnp.bfloat16)
-        out_copy(i).start()
-        return c
-
-    def out_wait(i, c):
-        out_copy(i).wait()
+        out_ref[:, cols] = o.astype(jnp.bfloat16)
         return c
 
     for hd in range(heads):
@@ -605,24 +594,16 @@
     for hd in range(heads):
         for t in others:
             att_copy(hd, t, h).wait_send()
-    lax.fori_loop(0, tiles, out_wait, 0)
-
-
-def hand_over(src, dst, held, in_sem, out_sem):
+
+
+def hand_over(src, dst, sem):
     rows = src.shape[0] // 8
-
-    def arrive(i):
-        span = pl.ds(i * rows, rows)
-        return pltpu.make_async_copy(src.at[span], held.at[span], in_sem.at[i])
 
     def leave(i):
         span = pl.ds(i * rows, rows)
-        return pltpu.make_async_copy(held.at[span], dst.at[span], out_sem.at[i])
+        return pltpu.make_async_copy(src.at[span], dst.at[span], sem.at[i])
 
     for i in range(8):
-        arrive(i).start()
-    for i in range(8):
-        arrive(i).wait()
         leave(i).start()
     for i in range(8):
         leave(i).wait()
@@ -639,22 +620,21 @@
     width = w_out.shape[1]
     kv = keys_values.reshape(blocks, BLOCK, 2, feat)
     anywhere = pl.BlockSpec(memory_space=pl.ANY)
+    vmem = pl.BlockSpec(memory_space=pltpu.VMEM)
     bf16, f32, i32 = jnp.bfloat16, jnp.float32, jnp.int32
     rows_out = tok_rows // n_head
     dma = pltpu.SemaphoreType.DMA
     mixed = pl.pallas_call(
         functools.partial(kernel, n, slots, blocks, heads),
-        out_shape=jax.ShapeDtypeStruct((rows_out, width), bf16),
+        out_shape=pltpu.VMEM((rows_out, width), bf16),
         in_specs=[anywhere, anywhere, pl.BlockSpec(memory_space=pltpu.SMEM), anywhere],
-        out_specs=anywhere,
+        out_specs=vmem,
         scratch_shapes=[
             pltpu.VMEM((tok_rows, feat), bf16),
             pltpu.VMEM((blocks, BLOCK, 2, feat), bf16),
             pltpu.VMEM((blocks, BLOCK, 2 * feat), bf16),
             pltpu.VMEM((8, 128), i32),
-            pltpu.VMEM((rows_out, width), bf16),
             dma((2,)),
-            dma((width // 512,)),
             pltpu.VMEM((blocks + 2, BLOCK, 2 * feat), bf16),
             pltpu.VMEM((2, BLOCK, 2 * feat), bf16),
             pltpu.VMEM((n * 8 + entries, 128), i32),
@@ -693,7 +673,7 @@
             dma((heads * n_head,)),
         ],
         compiler_params=pltpu.CompilerParams(
-            collective_id=0, has_side_effects=True, vmem_limit_bytes=60 * 1024 * 1024
+            collective_id=0, has_side_effects=True, vmem_limit_bytes=56 * 1024 * 1024
         ),
         cost_estimate=pl.CostEstimate(
             flops=6_000_000_000, bytes_accessed=20_000_000, transcendentals=2_000_000
@@ -702,9 +682,9 @@
     return pl.pallas_call(
         hand_over,
         out_shape=jax.ShapeDtypeStruct((rows_out, width), bf16),
-        in_specs=[anywhere],
+        in_specs=[vmem],
         out_specs=anywhere,
-        scratch_shapes=[pltpu.VMEM((rows_out, width), bf16), dma((8,)), dma((8,))],
+        scratch_shapes=[dma((8,))],
     )(mixed)
 
 

time: 118 us -> 119 us (level)
  local copies, waits for them, and re-layouts: 0 us -> 1.34 us
    unnamed x0 -> x2, local copies, waits for them, and re-layouts: none -> 1.34 us
where the time goes in v8:
time: 119 us
  Pallas kernels  117 us (98%)
  local copies, waits for them, and re-layouts  1.34 us (1%)
    pallas_call x1, Pallas kernels, body(): pl.pallas_call(functools.partial(kernel, n, slots, blocks, heads), out_sh...  114 us
    pallas_call x1, Pallas kernels, body(): pl.pallas_call(hand_over, out_shape=jax.ShapeDtypeStruct((rows_out, width...  2.96 us

profile of v8, /device:TPU:0, one launch (start us, length us, event | category | flops | bytes accessed | tf_op | source)
XLA Modules:
  0.0 118.6 jit_solution(12116951968261466123)
XLA Ops:
  0.0 114.3 %shard_map.46.src = bf16[256,4096]{1,0:T(8,128)(2,1)S(1)} custom-call(bf16[1024,512]{1,0:T(8,128)(2,1)} %q_hbm.1, bf16[16,64,2,512]{3,2,1,0:T(2,128)(2,1)} %bitcast.2, s32[2,16]{1,0:T(2,128)} %bitcast.3, bf16[512,4096]{1,0:T(8,128)(2,1)} %w_ref.1), custom_call_target="tpu_custom_call" | custom-call | flops 6000000000 | bytes 20000000 | tf_op jit(solution)/shard_map/pallas_call | solution.py:627
  114.3 0.0 copy-start
  114.3 1.3 %copy-done = bf16[256,4096]{1,0:T(8,128)(2,1)} copy-done((bf16[256,4096]{1,0:T(8,128)(2,1)}, bf16[256,4096]{1,0:T(8,128)(2,1)S(1)}, u32[]{:S(2)}) %copy-start) | copy-done | bytes 2097176
  115.7 3.0 %shard_map.47 = bf16[256,4096]{1,0:T(8,128)(2,1)} custom-call(bf16[256,4096]{1,0:T(8,128)(2,1)} %copy-done), custom_call_target="tpu_custom_call" | custom-call | tf_op jit(solution)/shard_map/pallas_call | solution.py:682
Async XLA Ops:
  114.3 1.3 %copy-start = (bf16[256,4096]{1,0:T(8,128)(2,1)}, bf16[256,4096]{1,0:T(8,128)(2,1)S(1)}, u32[]{:S(2)}) copy-start(bf16[256,4096]{1,0:T(8,128)(2,1)S(1)} %shard_map.46.src) | copy-start | bytes 6291460
